TPU v7x, 512 devices: a whole 4x8x8 slice. The times are simulated.
512 devices in a mesh: row: 16 (over y, core), col: 32 (over z, x).
Axes of the slice: x: 4, y: 8, z: 8, core: 2. Of those that a mesh axis runs over, the one named last changes fastest.
Arguments:
- covariance: float32 [16384, 16384], P('row', 'col'), may hold values from -80 to 80, as said below
Outputs:
- factored: float32 [16384, 16384], P('row', 'col')
Inputs may be any that keep to these rules, and one draw needn't show every extreme that they name: covariance holds, in the storage order of the first step, a symmetric positive definite matrix whose eigenvalues are at least a quarter of its smallest diagonal entry.
All inputs are finite; a program needn't handle non-finite values.
Results may differ from a plain program's by a relative error of at most 0.0003.
Values sent between devices are 32-bit elements; how exact they have to be, the bound alone decides.
No kernel may reach another device: no remote copies, remote signals or barrier semaphores. Data moves between devices by JAX's collectives and lax.ppermute only.
A program may use at most 64 MiB of HBM per device.

v0:
```python
import jax
import jax.numpy as jnp
from jax import lax
from jax.sharding import PartitionSpec as P

NB = 512


HIGH = lax.Precision.HIGHEST


def spread(value, axis, source):
    kept = jnp.where(lax.axis_index(axis) == source, value, 0).astype(value.dtype)
    return lax.psum(kept, axis)


def right_solve(values, inverse):
    return lax.dot_general(values, inverse, (((1,), (1,)), ((), ())), precision=HIGH)


def body(covariance):
    nrows = lax.axis_size("row")
    ncols = lax.axis_size("col")
    row_here = lax.axis_index("row")
    col_here = lax.axis_index("col")
    local_rows, local_cols = covariance.shape
    group = ncols // nrows
    row_tile = jnp.arange(local_rows, dtype=jnp.int32) // NB * nrows + row_here
    col_tile = jnp.arange(local_cols, dtype=jnp.int32) // NB * ncols + col_here
    state = covariance
    own_col = 0 % ncols
    col_spot = 0 // ncols * NB
    own_row = 0 % nrows
    row_spot = 0 // nrows * NB
    slab = state
    panel = spread(slab, "col", own_col)
    block = spread(panel[row_spot : row_spot + NB], "row", own_row)
    factor = jnp.linalg.cholesky(block)
    inverse = lax.linalg.triangular_solve(
        factor, jnp.eye(NB, dtype=state.dtype), left_side=True, lower=True
    )
    solved = right_solve(panel, inverse)
    repeated = jnp.tile(factor, (local_rows // NB, 1))
    lower = jnp.where(
        (row_tile > 0)[:, None],
        solved,
        jnp.where((row_tile == 0)[:, None], repeated, jnp.zeros_like(solved)),
    )
    blocks = lower.reshape(local_cols // NB, group, NB, NB)
    picked = lax.dynamic_slice_in_dim(blocks, col_here // nrows, 1, 1).reshape(local_cols, NB)
    mirror = spread(picked, "row", col_here % nrows)
    update = state - lax.dot_general(lower, mirror, (((1,), (1,)), ((), ())), precision=HIGH)
    inside = (row_tile > 0)[:, None] & (col_tile > 0)[None, :]
    trailing = jnp.where(inside, update, jnp.zeros_like(update))
    fresh = jnp.where((col_tile > 0)[None, :], trailing, state)
    placed = jnp.where(col_here == own_col, lower, fresh)
    state = fresh.at[:, col_spot : col_spot + NB].set(placed)
    return state


def solution(mesh):
    return jax.shard_map(
        body,
        mesh=mesh,
        in_specs=(P("row", "col"),),
        out_specs=P("row", "col"),
        check_vma=False,
    )
```

profile of v0, /device:TPU:1, one launch (start us, length us, event | category | flops | bytes accessed | tf_op | source)
XLA Modules:
  0.0 609.0 jit_solution(11825626876032826107)
XLA Ops:
  6.5 1.9 copy.2
  8.5 1.6 broadcast_select_fusion.1
  10.2 167.9 %all-reduce.5.cloned.1.call-done = f32[1024,512]{0,1:T(8,128)} async-done(((f32[1024,512]{0,1:T(8,128)}), f32[1024,512]{0,1:T(8,128)}) %all-reduce.5.cloned.1.call-update) | async-done | bytes 2097168 | tf_op jit(solution)/shard_map/psum | solution.py:14
  178.0 2.3 slice_select_fusion
  181.0 0.8 iota_compare_fusion
  181.8 1.1 fusion.17
  182.9 115.1 %all-reduce.7.cloned.1.call-done = f32[512,512]{0,1:T(8,128)} async-done(((f32[512,512]{0,1:T(8,128)}), f32[512,512]{0,1:T(8,128)}) %all-reduce.7.cloned.1.call-update) | async-done | bytes 1048592 | tf_op jit(solution)/shard_map/psum | solution.py:14
  298.0 2.6 copy.3
  300.6 1.4 fusion.7
  302.1 1.0 copy-done.4
  303.1 11.7 %cholesky.103 = f32[128,128]{1,0:T(8,128)S(1)} custom-call(f32[128,128]{1,0:T(8,128)S(1)} %cholesky.263), custom_call_target="Cholesky" | custom-call | tf_op jit(solution)/shard_map/jit(cholesky)/cholesky | solution.py:38
  314.8 9.8 %custom-call.30 = f32[1,128,128]{1,2,0:T(8,128)S(1)} custom-call(f32[1,128,128]{2,1,0:T(8,128)S(1)} %get-tuple-element.54), custom_call_target="InvertDiagBlocksLowerTriangular" | custom-call | tf_op jit(solution)/shard_map/jit(cholesky)/cholesky | solution.py:38
  324.6 1.2 fusion.23
  325.9 1.3 convolution_subtract_fusion.3
  327.2 11.7 %cholesky.215 = f32[128,128]{1,0:T(8,128)S(1)} custom-call(f32[128,128]{1,0:T(8,128)S(1)} %cholesky.267), custom_call_target="Cholesky" | custom-call | tf_op jit(solution)/shard_map/jit(cholesky)/cholesky | solution.py:38
  338.9 0.7 copy.6
  339.8 0.7 copy.4
  340.5 10.6 %custom-call.31 = f32[1,128,128]{1,2,0:T(8,128)} custom-call(f32[1,128,128]{2,1,0:T(8,128)S(1)} %get-tuple-element.52), custom_call_target="InvertDiagBlocksLowerTriangular" | custom-call | tf_op jit(solution)/shard_map/jit(cholesky)/cholesky | solution.py:38
  351.1 1.0 cholesky.222
  352.0 0.8 constant_dynamic-update-slice_fusion.2
  352.9 1.2 convolution_dynamic-update-slice_fusion
  354.0 1.5 convolution_subtract_fusion.4
  355.6 11.7 %cholesky.236 = f32[128,128]{1,0:T(8,128)S(1)} custom-call(f32[128,128]{1,0:T(8,128)S(1)} %cholesky.272), custom_call_target="Cholesky" | custom-call | tf_op jit(solution)/shard_map/jit(cholesky)/cholesky | solution.py:38
  367.4 9.8 %custom-call.32 = f32[1,128,128]{1,2,0:T(8,128)S(1)} custom-call(f32[1,128,128]{2,1,0:T(8,128)S(1)} %get-tuple-element.50), custom_call_target="InvertDiagBlocksLowerTriangular" | custom-call | tf_op jit(solution)/shard_map/jit(cholesky)/cholesky | solution.py:38
  377.5 1.3 convolution_subtract_fusion.5
  378.9 11.9 %cholesky.253 = f32[128,128]{1,0:T(8,128)S(1)} custom-call(f32[128,128]{1,0:T(8,128)S(1)} %convolution_subtract_fusion.5), custom_call_target="Cholesky" | custom-call | tf_op jit(solution)/shard_map/jit(cholesky)/cholesky | solution.py:38
  391.5 0.6 compare_reduce_fusion
  392.2 0.7 compare_reduce_fusion.2
  395.4 1.6 fusion.8
  397.0 14.7 %while.3 = (s32[]{:T(128)}, f32[512,512]{0,1:T(8,128)}, s32[4,2]{0,1:T(2,128)S(1)}, f32[4,128,128]{2,1,0:T(8,128)}, s32[]{:T(128)}) while((s32[]{:T(128)}, f32[512,512]{0,1:T(8,128)}, s32[4,2]{0,1:T(2,128)S(1)}, f32[4,128,128]{2,1,0:T(8,128)}, s32[]{:T(128)}) %tuple.33), condition=%wide.while_cond.1, body=%wide.while_body.1.sunk | while | flops 2 | bytes 393829 | solution.py:39
  397.6 2.3 dynamic-slice.12
  401.3 2.3 dynamic-slice.12
  405.0 2.3 dynamic-slice.12
  408.7 2.2 dynamic-slice.12
  411.7 40.1 %custom-call.33 = f32[4,128,128]{1,2,0:T(8,128)S(1)} custom-call(f32[4,128,128]{2,1,0:T(8,128)} %get-tuple-element.32), custom_call_target="InvertDiagBlocksLowerTriangular" | custom-call | tf_op jit(solution)/shard_map/triangular_solve | solution.py:39
  451.8 1.1 fusion.19
  452.9 1.4 convolution_subtract_fusion.1
  454.8 1.4 convolution_subtract_fusion
  456.6 1.6 convolution_subtract_fusion.2
  458.6 0.7 tile.4
  459.8 1.1 copy-done
  460.9 5.0 select_select_fusion.1
  465.9 4.3 reshape.106
  470.2 2.7 broadcast_select_fusion
  472.9 1.1 copy.25
  474.0 117.5 %all-reduce.9.cloned.1.call-done = f32[512,512]{0,1:T(8,128)} async-done(((f32[512,512]{0,1:T(8,128)}), f32[512,512]{0,1:T(8,128)}) %all-reduce.9.cloned.1.call-update) | async-done | bytes 1048592 | tf_op jit(solution)/shard_map/psum | solution.py:14
  591.5 7.7 %select_select_fusion = f32[1024,512]{0,1:T(8,128)} fusion(f32[1024,512]{0,1:T(8,128)} %select_select_fusion.1, f32[1024,512]{0,1:T(8,128)S(1)} %copy.2, f32[512,512]{0,1:T(8,128)} %all-reduce.9.cloned.1.call-done, pred[1024]{0:T(1024)(128)(4,1)S(1)} %get-tuple-element.56, pred[]{:T(512)S(6)} %eq.28, pred[512]{0:T(512)(128)(4,1)S(1)} %fusion.46), kind=kOutput, calls=%fused_computation.2 | convolution fusion | flops 3223846912 | bytes 7341569 | tf_op jit(solution)/shard_map/dot_general | solution.py:52
  599.2 2.9 copy.16
  (56 shorter events, 9.4 us)
Async XLA Ops:
  6.5 171.5 %all-reduce.5.cloned.1.call-start = ((), (), s32[]{:S(2)}) async-start(), calls=%async_computation | async-start | bytes 4194304 | tf_op jit(solution)/shard_map/psum | solution.py:14
  10.1 287.9 %all-reduce.7.cloned.1.call-start = ((), (), s32[]{:S(2)}) async-start(), calls=%async_computation.1 | async-start | bytes 2097152 | tf_op jit(solution)/shard_map/psum | solution.py:14
  180.3 411.1 %all-reduce.9.cloned.1.call-start = ((), (), s32[]{:S(2)}) async-start(), calls=%async_computation.2 | async-start | bytes 2097152 | tf_op jit(solution)/shard_map/psum | solution.py:14
  298.0 2.6 copy-start.1
  302.1 1.0 copy-start.4
  367.4 29.6 %copy-start.5 = (s32[4]{0:T(128)S(1)}, s32[4]{0:T(128)}, u32[]{:S(2)}) copy-start(s32[4]{0:T(128)} %iota_multiply_fusion) | copy-start | bytes 52
  397.0 57.8 %copy-start.3 = (f32[512,512]{1,0:T(8,128)S(1)}, f32[512,512]{1,0:T(8,128)}, u32[]{:S(2)}) copy-start(f32[512,512]{1,0:T(8,128)} %fusion.17) | copy-start | bytes 3145732
  454.3 4.3 copy-start.2
  459.4 1.6 copy-start
Sparse Core Ops, SparseCore 0:
  10.9 167.1 all-reduce.4
  180.5 117.4 all-reduce.6
  474.1 117.3 all-reduce.8
where the time goes:
time: 619 us; the launch traced here: 609 us
  waiting for transfers between devices  401 us (65%)
  other arithmetic  132 us (21%)
  local copies, waits for them, and re-layouts  34.3 us (6%)
  matrix products  26.2 us (4%)
  between operations  16.4 us (3%)
    psum x3, waiting for transfers between devices, spread(): return lax.psum(kept, axis)  400 us
    another operation x14, other arithmetic, body(): factor = jnp.linalg.cholesky(block)  79.3 us
    another operation x3, other arithmetic, body(): lax.linalg.triangular_solve(factor, jnp.eye(NB, dtype=state.dtype), left_...  42.3 us
    another operation x20, local copies, waits for them, and re-layouts  14.6 us
  transfers between devices with their start and end apart: 3, of which 3 were waited for; matrix products, arithmetic and copies ran while one was open for 0% of the time, Pallas kernels for 0%

commit v1 on v0

v1 whole, which is shorter than its diff:
```python
import functools

import jax
import jax.numpy as jnp
from jax import lax
from jax.experimental import pallas as pl
from jax.experimental.pallas import tpu as pltpu
from jax.sharding import Mesh
from jax.sharding import PartitionSpec as P

NB = 512
BK = 128
SUB = 8
CHUNK = 256
HIGH = lax.Precision.HIGHEST


def _rows(value, m):
    return jnp.broadcast_to(value[m : m + 1, :], (SUB, BK))


def _lanes(value, m):
    return jnp.broadcast_to(value[:, m : m + 1], (SUB, BK))


def _small_inverse(rows):
    lane = lax.broadcasted_iota(jnp.int32, (SUB, BK), 1)
    sub = lax.broadcasted_iota(jnp.int32, (SUB, BK), 0)
    rows = list(rows)
    n = len(rows)
    out = []
    for k in range(n):
        base = SUB * k
        pivot = (lane >= base) & (lane < base + SUB)
        p = [_rows(rows[k], m) for m in range(SUB)]
        c = [[_lanes(p[m], base + l) if l >= m else None for l in range(SUB)] for m in range(SUB)]
        p = [
            jnp.where(pivot, jnp.where(lane == base + m, 1.0, 0.0), p[m]) for m in range(SUB)
        ]
        if k + 1 < n:
            g = [_lanes(rows[k + 1], base + m) for m in range(SUB)]
            ahead = jnp.where(pivot, 0.0, rows[k + 1])
        f = [[None] * SUB for _ in range(SUB)]
        inv = []
        for j in range(SUB):
            inv.append(pl.reciprocal(c[j][j], approx=True))
            for l in range(j + 1, SUB):
                f[j][l] = c[j][l] * inv[j]
                for l2 in range(l, SUB):
                    c[l][l2] = c[l][l2] - f[j][l] * c[j][l2]
            for l in range(j + 1, SUB):
                p[l] = p[l] - f[j][l] * p[j]
            if k + 1 < n:
                h = g[j] * inv[j]
                ahead = ahead - h * p[j]
                for l in range(j + 1, SUB):
                    g[l] = g[l] - h * c[j][l]
        done = p[0] * lax.rsqrt(c[0][0])
        for m in range(1, SUB):
            done = jnp.where(sub == m, p[m] * lax.rsqrt(c[m][m]), done)
        out.append(jnp.where(lane <= sub + base, done, 0.0))
        if k + 1 < n:
            rows[k + 1] = ahead
        if k + 2 < n:
            s = [p[m] * inv[m] for m in range(SUB)]
            for l in range(SUB - 1, 0, -1):
                for j in range(l):
                    s[j] = s[j] - f[j][l] * s[l]
            for i in range(k + 2, n):
                parts = [_lanes(rows[i], base + m) * s[m] for m in range(SUB)]
                while len(parts) > 1:
                    parts = [a + b for a, b in zip(parts[::2], parts[1::2])]
                rows[i] = jnp.where(pivot, 0.0, rows[i]) - parts[0]
    return out


def _dot(a, b):
    return lax.dot_general(
        a,
        b,
        (((1,), (0,)), ((), ())),
        precision=HIGH,
        preferred_element_type=jnp.float32,
    )


def _eliminate(k, v_ref):
    here = slice(k * BK, (k + 1) * BK)
    rows = [v_ref[k * BK + SUB * i : k * BK + SUB * (i + 1), here] for i in range(BK // SUB)]
    small = jnp.concatenate(_small_inverse(rows), axis=0)
    v_ref[here, :] = _dot(small, v_ref[here, :])
    v_ref[here, here] = small
    for i in range(k + 1, NB // BK):
        there = slice(i * BK, (i + 1) * BK)
        v_ref[there, here] = jnp.zeros((BK, BK), jnp.float32)
        v_ref[there, :] -= _dot(v_ref[here, there].T, v_ref[here, :])


def _first_kernel(here_ref, mine_ref, other_ref, v_ref):
    half = NB // 2

    @pl.when(here_ref[2] == 0)
    def _():
        v_ref[:half, :] = mine_ref[...]
        v_ref[half:, :] = other_ref[...]

    @pl.when(here_ref[2] != 0)
    def _():
        v_ref[:half, :] = other_ref[...]
        v_ref[half:, :] = mine_ref[...]

    _eliminate(0, v_ref)


def _next_kernel(k, old_ref, v_ref):
    v_ref[...] = old_ref[...]
    _eliminate(k, v_ref)


def _handing_kernel(old_ref, _, v_ref, __):
    _next_kernel(1, old_ref, v_ref)


def factor_inverse(here, mine, other, own):
    vmem = pl.BlockSpec(memory_space=pltpu.VMEM)
    rest = dict(
        out_shape=jax.ShapeDtypeStruct((NB, NB), jnp.float32),
        out_specs=vmem,
        compiler_params=pltpu.CompilerParams(vmem_limit_bytes=24 * 2**20),
        cost_estimate=pl.CostEstimate(
            flops=8 * 10**9, bytes_accessed=8 * NB * NB, transcendentals=NB
        ),
    )
    state = pl.pallas_call(
        _first_kernel,
        in_specs=[pl.BlockSpec(memory_space=pltpu.SMEM), vmem, vmem],
        name="factor_0",
        **rest,
    )(here, mine, other)
    handed = dict(
        rest,
        out_shape=(rest["out_shape"], jax.ShapeDtypeStruct(own.shape, own.dtype)),
        out_specs=(vmem, pl.BlockSpec(memory_space=pl.ANY)),
        input_output_aliases={1: 1},
    )
    for k in range(1, NB // BK):
        if k == 1:
            state, own = pl.pallas_call(
                _handing_kernel,
                in_specs=[vmem, pl.BlockSpec(memory_space=pl.ANY)],
                name="factor_1",
                **handed,
            )(state, own)
        else:
            state = pl.pallas_call(
                functools.partial(_next_kernel, k), in_specs=[vmem], name=f"factor_{k}", **rest
            )(state)
    return state, own


def _split(value):
    top = value.astype(jnp.bfloat16)
    return top, (value - top.astype(jnp.float32)).astype(jnp.bfloat16)


def _dot3(a, b, dims):
    return sum(
        lax.dot_general(x, y, (dims, ((), ())), preferred_element_type=jnp.float32)
        for x, y in ((a[1], b[0]), (a[0], b[1]), (a[0], b[0]))
    )


def _update_kernel(
    here_ref, state_ref, own_ref, back_ref, top_ref, low_ref, ahead_ref, tile_ref, inverse_ref,
    o_ref, panel_ref, inv_ref, mirror_ref,
):
    row, col, x = here_ref[0], here_ref[1], here_ref[3]
    i = pl.program_id(0)
    first = pl.multiple_of(i * CHUNK, CHUNK)
    half = CHUNK // 2

    @pl.when(i == 0)
    def _():
        for k in range(NB // BK):
            here = slice(k * BK, (k + 1) * BK)
            wide = inverse_ref[here, :]
            lane = lax.broadcasted_iota(jnp.int32, wide.shape, 1)
            top, low = _split(jnp.where(lane < (k + 1) * BK, wide, 0.0))
            inv_ref[0, here, :] = top
            inv_ref[1, here, :] = low

        mirror = _split(_dot3((inv_ref[0], inv_ref[1]), _split(tile_ref[...]), ((1,), (0,))))
        mirror_ref[0] = mirror[0]
        mirror_ref[1] = mirror[1]

    turn = lax.rem(x + 4 - i, 4)
    for j, part in ((0, own_ref), (1, back_ref), (3, ahead_ref)):

        @pl.when(turn == j)
        def _():
            panel_ref[...] = part[...]

    @pl.when(turn == 2)
    def _():
        panel_ref[:half, :] = top_ref[...]
        panel_ref[half:, :] = low_ref[...]

    solved = _dot3(_split(panel_ref[...]), (inv_ref[0], inv_ref[1]), ((1,), (1,)))
    top = (row == 0) & (first < NB)

    @pl.when(col == 0)
    def _():
        r = lax.broadcasted_iota(jnp.int32, solved.shape, 0) + first
        c = lax.broadcasted_iota(jnp.int32, solved.shape, 1)
        o_ref[...] = jnp.where(top & (c > r), 0.0, solved)

    @pl.when(col != 0)
    def _():
        new = state_ref[...] - _dot3(_split(solved), (mirror_ref[0], mirror_ref[1]), ((1,), (0,)))
        o_ref[...] = jnp.where(top, 0.0, new)


def update(here, state, panel, mirror, inverse):
    block = pl.BlockSpec((CHUNK, NB), lambda i: (i, 0))
    vmem = pl.BlockSpec(memory_space=pltpu.VMEM)
    return pl.pallas_call(
        _update_kernel,
        grid=(state.shape[0] // CHUNK,),
        out_shape=jax.ShapeDtypeStruct(state.shape, jnp.float32),
        in_specs=[pl.BlockSpec(memory_space=pltpu.SMEM), block] + [vmem] * 7,
        out_specs=block,
        scratch_shapes=[
            pltpu.VMEM((CHUNK, NB), jnp.float32),
            pltpu.VMEM((2, NB, NB), jnp.bfloat16),
            pltpu.VMEM((2, NB, NB), jnp.bfloat16),
        ],
        compiler_params=pltpu.CompilerParams(vmem_limit_bytes=40 * 2**20),
        cost_estimate=pl.CostEstimate(
            flops=30 * NB**3, bytes_accessed=32 * NB * NB, transcendentals=0
        ),
        name="update",
    )(here, state, *panel, mirror, inverse)


def send_parts(value, axis, parts):
    size = value.shape[0] // parts
    return lax.all_to_all(value.reshape(parts, size, value.shape[1]), axis, 0, 0)[0]


def gather(value, axis, parts):
    copies = jnp.broadcast_to(value[None], (parts,) + value.shape)
    return lax.all_to_all(copies, axis, 0, 0).reshape(-1, value.shape[1])


def swap_cores(value):
    return lax.ppermute(value, "core", [(0, 1), (1, 0)])


def body(covariance):
    ny, nz, nx = (lax.axis_size(axis) for axis in ("y", "z", "x"))
    core, x, y, z = (lax.axis_index(axis) for axis in ("core", "x", "y", "z"))
    half = NB // 2
    here = jnp.stack([y * 2 + core, z * nx + x, core, x]).astype(jnp.int32)

    tile = covariance[:NB]
    mine = jnp.where(core == 0, tile[:half], swap_cores(tile[half:]))

    part = send_parts(mine, ("z", "x"), nz * nx)
    part = gather(part, "y", ny)[: part.shape[0]]
    diagonal = gather(part, ("z", "x"), nz * nx)

    size = covariance.shape[0] // nx
    quarter = jnp.where(x == 0, covariance[:size], 0.0)
    for i in range(1, nx):
        quarter = quarter + lax.ppermute(
            covariance[i * size : (i + 1) * size], ("z", "x"), [(0, i)]
        )
    spread = lax.ppermute(quarter, "z", [(0, 3)]) + lax.ppermute(quarter, "z", [(0, 5)])
    spread = jnp.where(z == 0, quarter, spread)
    own = lax.ppermute(spread, "z", [(0, 1), (3, 4), (5, 6)])
    own = own + lax.ppermute(spread, "z", [(0, 7), (3, 2)])
    own = jnp.where((z == 0) | (z == 3) | (z == 5), spread, own)

    inverse, own = factor_inverse(here, diagonal, swap_cores(diagonal), own)

    ring = [(i, (i + 1) % nx) for i in range(nx)]
    back_ring = [(j, i) for i, j in ring]
    back = lax.ppermute(own, "x", ring)
    ahead = lax.ppermute(own, "x", back_ring)
    top = lax.ppermute(back[: size // 2], "x", ring)
    low = lax.ppermute(ahead[size // 2 :], "x", back_ring)

    mirror = tile
    for step in (4, 2, 1):
        pairs = [(2 * i, 2 * (i + step)) for i in range(0, ny, 2 * step)]
        sent = lax.ppermute(mirror, ("y", "core"), pairs)
        mirror = jnp.where(y % (2 * step) == step, sent, mirror)
    mirror = jnp.where(core == 0, mirror, lax.ppermute(mirror, "core", [(0, 1)]))
    return update(here, covariance, (own, back, top, low, ahead), mirror, inverse)


def solution(mesh):
    fine = Mesh(mesh.devices.reshape(8, 2, 8, 4), ("y", "core", "z", "x"))
    spec = P(("y", "core"), ("z", "x"))
    return jax.shard_map(body, mesh=fine, in_specs=(spec,), out_specs=spec, check_vma=False)
```

time: 619 us -> 153 us (0.25)
  the two profiles are of different devices: /device:TPU:1 before, /device:TPU:64 now
where the time goes in v1:
time: 153 us; the launch traced here: 152 us
  starting transfers between devices  75.5 us (49%)
  waiting for transfers between devices  31.9 us (21%)
  Pallas kernels  28.8 us (19%)
  other arithmetic  10.4 us (7%)
  local copies, waits for them, and re-layouts  5.2 us (3%)
    ppermute x3, starting transfers between devices, body(): sent = lax.ppermute(mirror, ('y', 'core'), pairs)  17.7 us
    all_to_all x1, starting transfers between devices, send_parts(): lax.all_to_all(value.reshape(parts, size, value.shape[1]), axis, 0, 0)[0]  15.9 us
    all_to_all x2, starting transfers between devices, gather(): return lax.all_to_all(copies, axis, 0, 0).reshape(-1, value.shape[1])  14 us
    all_to_all x2, waiting for transfers between devices, gather(): return lax.all_to_all(copies, axis, 0, 0).reshape(-1, value.shape[1])  11 us
    pallas_call x2, Pallas kernels, factor_inverse(): pl.pallas_call(functools.partial(_next_kernel, k), in_specs=[vmem], name=...  9.72 us
    all_to_all x1, waiting for transfers between devices, send_parts(): lax.all_to_all(value.reshape(parts, size, value.shape[1]), axis, 0, 0)[0]  8.06 us
    pallas_call x1, Pallas kernels, update(): pl.pallas_call(_update_kernel, grid=(state.shape[0] // CHUNK,), out_shape...  7.37 us
    pallas_call x1, Pallas kernels, factor_inverse(): pl.pallas_call(_first_kernel, in_specs=[pl.BlockSpec(memory_space=pltpu.S...  6.41 us
  transfers between devices with their start and end apart: 20, of which 6 were waited for; matrix products, arithmetic and copies ran while one was open for 9% of the time, Pallas kernels for 14%

profile of v1, /device:TPU:64, one launch (start us, length us, event | category | flops | bytes accessed | tf_op | source)
XLA Modules:
  0.0 152.2 jit_solution(9698890052325128398)
XLA Ops:
  0.0 2.6 %fusion = (f32[256,512]{1,0:T(8,128)}, f32[256,512]{1,0:T(8,128)}, f32[256,512]{1,0:T(8,128)S(1)}) fusion(f32[1024,512]{1,0:T(8,128)} %state_ref.1), kind=kLoop, calls=%fused_computation.11 | loop fusion | bytes 3145728 | tf_op jit(solution)/shard_map/slice | solution.py:276
  2.6 0.7 collective-permute-start.3
  3.3 1.5 collective-permute-start.4
  4.8 1.4 collective-permute-start.2
  6.2 1.9 %collective-permute-start = (f32[256,512]{1,0:T(8,128)S(1)}, f32[256,512]{1,0:T(8,128)}, u32[]{:S(2)}, u32[]{:S(2)}) collective-permute-start(f32[256,512]{1,0:T(8,128)S(1)} %get-tuple-element.13), channel_id=1, source_target_pairs={{0,32},{32,0},{1,33},{33,1},{2,34},{34,2},{3,35},{35,3},{4,36},{36... | collective-permute-start | bytes 1572872 | tf_op jit(solution)/shard_map/ppermute | solution.py:256
  8.1 1.0 slice.40
  9.2 8.7 %collective-permute-start.13 = (f32[512,512]{1,0:T(8,128)}, f32[512,512]{1,0:T(8,128)}, u32[]{:S(2)}, u32[]{:S(2)}) collective-permute-start(f32[512,512]{1,0:T(8,128)} %slice.40), channel_id=1, source_target_pairs={{0,256},{1,257},{2,258},{3,259},{4,260},{5,261},{6,262},{7,263},{8... | collective-permute-start | bytes 3145736 | tf_op jit(solution)/shard_map/ppermute | solution.py:296
  17.9 0.0 collective-permute-done
  17.9 2.3 %add_add_fusion = (f32[256,512]{1,0:T(8,128)S(1)}, f32[32,8,512]{2,1,0:T(8,128)}) fusion(f32[256,512]{1,0:T(8,128)} %collective-permute-done.4, f32[256,512]{1,0:T(8,128)S(1)} %collective-permute-done.3, f32[256,512]{1,0:T(8,128)} %collective-permute-done.2, f32[1024,512]{1,0:T(8,128)S(1)} %copy-done, pred[]{:T(512)S(6)} %eq.34, ...), kind=kLoop, calls=%fused_computation.2 | loop fusion | flops 655360 | bytes 3670018 | tf_op jit(solution)/shard_map/add | solution.py:275
  20.2 15.9 %all-to-all-start = ((f32[32,8,512]{2,1,0:T(8,128)}), f32[32,8,512]{2,1,0:T(8,128)S(1)}, u32[]{:S(2)}, u32[]{:S(2)}) async-start(f32[32,8,512]{2,1,0:T(8,128)} %get-tuple-element.10), calls=%async_computation | async-start | bytes 1048576 | tf_op jit(solution)/shard_map/all_to_all | solution.py:247
  36.1 1.2 broadcast_select_fusion
  37.3 5.5 %collective-permute-start.14 = (f32[512,512]{1,0:T(8,128)}, f32[512,512]{1,0:T(8,128)}, u32[]{:S(2)}, u32[]{:S(2)}) collective-permute-start(f32[512,512]{1,0:T(8,128)} %broadcast_select_fusion), channel_id=1, source_target_pairs={{0,128},{256,384},{1,129},{257,385},{2,130},{258,386},{3,131},{259... | collective-permute-start | bytes 3145736 | tf_op jit(solution)/shard_map/ppermute | solution.py:296
  42.8 8.1 %all-to-all-done = f32[32,8,512]{2,1,0:T(8,128)S(1)} async-done(((f32[32,8,512]{2,1,0:T(8,128)}), f32[32,8,512]{2,1,0:T(8,128)S(1)}, u32[]{:S(2)}, u32[]{:S(2)}) %all-to-all-start) | async-done | bytes 524320 | tf_op jit(solution)/shard_map/all_to_all | solution.py:247
  50.9 0.7 broadcast_in_dim.20
  51.6 8.9 %all-to-all-start.1 = ((f32[8,8,512]{2,1,0:T(8,128)}), f32[8,8,512]{2,1,0:T(8,128)S(1)}, u32[]{:S(2)}, u32[]{:S(2)}) async-start(f32[8,8,512]{2,1,0:T(8,128)} %broadcast_in_dim.20), calls=%async_computation.1 | async-start | bytes 262144 | tf_op jit(solution)/shard_map/all_to_all | solution.py:252
  60.4 1.5 collective-permute-start.6
  61.9 1.5 collective-permute-start.5
  63.4 6.1 %all-to-all-done.1 = f32[8,8,512]{2,1,0:T(8,128)S(1)} async-done(((f32[8,8,512]{2,1,0:T(8,128)}), f32[8,8,512]{2,1,0:T(8,128)S(1)}, u32[]{:S(2)}, u32[]{:S(2)}) %all-to-all-start.1) | async-done | bytes 131104 | tf_op jit(solution)/shard_map/all_to_all | solution.py:252
  69.5 0.9 broadcast_in_dim.22
  70.4 5.1 %all-to-all-start.2 = ((f32[32,8,512]{2,1,0:T(8,128)}), f32[32,8,512]{2,1,0:T(8,128)S(1)}, u32[]{:S(2)}, u32[]{:S(2)}) async-start(f32[32,8,512]{2,1,0:T(8,128)} %broadcast_in_dim.22), calls=%async_computation.2 | async-start | bytes 1048576 | tf_op jit(solution)/shard_map/all_to_all | solution.py:252
  75.5 2.5 %broadcast_select_fusion.1 = f32[512,512]{1,0:T(8,128)} fusion(f32[512,512]{1,0:T(8,128)} %collective-permute-done.14, f32[512,512]{1,0:T(8,128)} %broadcast_select_fusion, pred[]{:T(512)S(6)} %eq.36), kind=kLoop, calls=%fused_computation.5 | loop fusion | flops 262144 | bytes 3145729 | tf_op jit(solution)/shard_map/jit(_where)/select_n | solution.py:297
  78.0 3.5 %collective-permute-start.15 = (f32[512,512]{1,0:T(8,128)}, f32[512,512]{1,0:T(8,128)}, u32[]{:S(2)}, u32[]{:S(2)}) collective-permute-start(f32[512,512]{1,0:T(8,128)} %broadcast_select_fusion.1), channel_id=1, source_target_pairs={{0,64},{128,192},{256,320},{384,448},{1,65},{129,193},{257,321},{3... | collective-permute-start | bytes 3145736 | tf_op jit(solution)/shard_map/ppermute | solution.py:296
  81.5 0.0 collective-permute-done.6
  81.5 0.0 collective-permute-done.5
  81.5 1.3 add_select_fusion.1
  82.8 1.5 collective-permute-start.8
  84.3 1.3 collective-permute-start.7
  85.6 0.1 pad_add_fusion.here_ref
  85.7 4.8 %all-to-all-done.2 = f32[32,8,512]{2,1,0:T(8,128)S(1)} async-done(((f32[32,8,512]{2,1,0:T(8,128)}), f32[32,8,512]{2,1,0:T(8,128)S(1)}, u32[]{:S(2)}, u32[]{:S(2)}) %all-to-all-start.2) | async-done | bytes 524320 | tf_op jit(solution)/shard_map/all_to_all | solution.py:252
  90.6 1.9 %collective-permute-start.1 = (f32[256,512]{1,0:T(8,128)S(1)}, f32[256,512]{1,0:T(8,128)S(1)}, u32[]{:S(2)}, u32[]{:S(2)}) collective-permute-start(f32[256,512]{1,0:T(8,128)S(1)} %bitcast.11), channel_id=1, source_target_pairs={{0,32},{32,0},{1,33},{33,1},{2,34},{34,2},{3,35},{35,3},{4,36},{36... | collective-permute-start | bytes 1572872 | tf_op jit(solution)/shard_map/ppermute | solution.py:256
  92.5 0.0 collective-permute-done.8
  92.5 5.5 %collective-permute-done.7 = f32[256,512]{1,0:T(8,128)} collective-permute-done((f32[256,512]{1,0:T(8,128)S(1)}, f32[256,512]{1,0:T(8,128)}, u32[]{:S(2)}, u32[]{:S(2)}) %collective-permute-start.7) | collective-permute-done | bytes 524320 | tf_op jit(solution)/shard_map/ppermute | solution.py:280
  98.0 1.3 add_select_fusion._
  99.4 0.0 collective-permute-done.15
  99.4 1.4 broadcast_select_fusion.2
  100.8 1.4 collective-permute-start.16
  102.2 6.4 %factor_0.1.old_ref = f32[512,512]{1,0:T(8,128)S(1)} custom-call(s32[4]{0:T(128)S(1)} %pad_add_fusion.here_ref, f32[256,512]{1,0:T(8,128)S(1)} %bitcast.12, f32[256,512]{1,0:T(8,128)S(1)} %collective-permute-done.1.other_ref), custom_call_target="tpu_custom_call" | custom-call | flops 8000000000 | bytes 2097152 | tf_op jit(solution)/shard_map/factor_0/pallas_call | solution.py:134
  108.6 5.3 %factor_1.1 = (f32[512,512]{1,0:T(8,128)S(1)}, f32[256,512]{1,0:T(8,128)S(1)}) custom-call(f32[512,512]{1,0:T(8,128)S(1)} %factor_0.1.old_ref, f32[256,512]{1,0:T(8,128)S(1)} %add_select_fusion._), custom_call_target="tpu_custom_call", output_to_operand_aliasing={{1}: (1, {})} | custom-call | flops 8000000000 | bytes 2097152 | tf_op jit(solution)/shard_map/factor_1/pallas_call | solution.py:148
  113.9 4.3 %collective-permute-start.11 = (f32[256,512]{1,0:T(8,128)S(1)}, f32[256,512]{1,0:T(8,128)S(1)}, u32[]{:S(2)}, u32[]{:S(2)}) collective-permute-start(f32[256,512]{1,0:T(8,128)S(1)} %get-tuple-element.7.own_ref), channel_id=1, source_target_pairs={{1,0},{2,1},{3,2},{0,3},{5,4},{6,5},{7,6},{4,7},{9,8},{10,9},{11,1... | collective-permute-start | bytes 1572872 | tf_op jit(solution)/shard_map/ppermute | solution.py:289
  118.2 2.1 %collective-permute-start.9 = (f32[256,512]{1,0:T(8,128)S(1)}, f32[256,512]{1,0:T(8,128)S(1)}, u32[]{:S(2)}, u32[]{:S(2)}) collective-permute-start(f32[256,512]{1,0:T(8,128)S(1)} %get-tuple-element.7.own_ref), channel_id=1, source_target_pairs={{0,1},{1,2},{2,3},{3,0},{4,5},{5,6},{6,7},{7,4},{8,9},{9,10},{10,1... | collective-permute-start | bytes 1572872 | tf_op jit(solution)/shard_map/ppermute | solution.py:288
  120.4 5.0 %factor_2.1.old_ref = f32[512,512]{1,0:T(8,128)S(1)} custom-call(f32[512,512]{1,0:T(8,128)S(1)} %get-tuple-element.8.old_ref), custom_call_target="tpu_custom_call" | custom-call | flops 8000000000 | bytes 2097152 | tf_op jit(solution)/shard_map/factor_2/pallas_call | solution.py:155
  125.4 4.7 %factor_3.1.inverse_ref = f32[512,512]{1,0:T(8,128)S(1)} custom-call(f32[512,512]{1,0:T(8,128)S(1)} %factor_2.1.old_ref), custom_call_target="tpu_custom_call" | custom-call | flops 8000000000 | bytes 2097152 | tf_op jit(solution)/shard_map/factor_3/pallas_call | solution.py:155
  130.1 5.1 %collective-permute-start.12 = (f32[128,512]{1,0:T(8,128)S(1)}, f32[128,512]{1,0:T(8,128)S(1)}, u32[]{:S(2)}, u32[]{:S(2)}) collective-permute-start(f32[128,512]{1,0:T(8,128)S(1)} %slice.44), channel_id=1, source_target_pairs={{1,0},{2,1},{3,2},{0,3},{5,4},{6,5},{7,6},{4,7},{9,8},{10,9},{11,1... | collective-permute-start | bytes 786440 | tf_op jit(solution)/shard_map/ppermute | solution.py:291
  135.3 1.9 %collective-permute-start.10 = (f32[128,512]{1,0:T(8,128)S(1)}, f32[128,512]{1,0:T(8,128)S(1)}, u32[]{:S(2)}, u32[]{:S(2)}) collective-permute-start(f32[128,512]{1,0:T(8,128)S(1)} %slice.43), channel_id=1, source_target_pairs={{0,1},{1,2},{2,3},{3,0},{4,5},{5,6},{6,7},{7,4},{8,9},{9,10},{10,1... | collective-permute-start | bytes 786440 | tf_op jit(solution)/shard_map/ppermute | solution.py:290
  137.3 0.2 broadcast_select_fusion.3.tile_ref
  137.5 1.7 %collective-permute-done.12.low_ref = f32[128,512]{1,0:T(8,128)S(1)} collective-permute-done((f32[128,512]{1,0:T(8,128)S(1)}, f32[128,512]{1,0:T(8,128)S(1)}, u32[]{:S(2)}, u32[]{:S(2)}) %collective-permute-start.12) | collective-permute-done | bytes 262176 | tf_op jit(solution)/shard_map/ppermute | solution.py:291
  139.2 5.6 %collective-permute-done.10.top_ref = f32[128,512]{1,0:T(8,128)S(1)} collective-permute-done((f32[128,512]{1,0:T(8,128)S(1)}, f32[128,512]{1,0:T(8,128)S(1)}, u32[]{:S(2)}, u32[]{:S(2)}) %collective-permute-start.10) | collective-permute-done | bytes 262176 | tf_op jit(solution)/shard_map/ppermute | solution.py:290
  144.8 7.4 %update.1 = f32[1024,512]{1,0:T(8,128)} custom-call(s32[4]{0:T(128)S(1)} %pad_add_fusion.here_ref, f32[1024,512]{1,0:T(8,128)S(1)} %copy-done, f32[256,512]{1,0:T(8,128)S(1)} %get-tuple-element.7.own_ref, f32[256,512]{1,0:T(8,128)S(1)} %collective-permute-done.9.back_ref, f32[128,512]{1,0:T(8,128)S(1)} %collective-permute-done.10.top_ref, ...), custom_call_target="tpu_custom_call" | custom-call | flops 4026531840 | bytes 8388608 | tf_op jit(solution)/shard_map/update/pallas_call | solution.py:226
  (19 shorter events, 0.1 us)
Async XLA Ops:
  0.0 8.1 %copy-start = (f32[1024,512]{1,0:T(8,128)S(1)}, f32[1024,512]{1,0:T(8,128)}, u32[]{:S(2)}) copy-start(f32[1024,512]{1,0:T(8,128)} %state_ref.1) | copy-start | bytes 6291460
  2.6 15.3 %collective-permute-start.3 = (f32[256,512]{1,0:T(8,128)}, f32[256,512]{1,0:T(8,128)S(1)}, u32[]{:S(2)}, u32[]{:S(2)}) collective-permute-start(f32[256,512]{1,0:T(8,128)} %get-tuple-element.11), channel_id=1, source_target_pairs={{0,2},{32,34},{64,66},{96,98},{128,130},{160,162},{192,194},{224,2... | collective-permute-start | bytes 1572872 | tf_op jit(solution)/shard_map/ppermute | solution.py:275
  3.3 14.6 %collective-permute-start.4 = (f32[256,512]{1,0:T(8,128)}, f32[256,512]{1,0:T(8,128)}, u32[]{:S(2)}, u32[]{:S(2)}) collective-permute-start(f32[256,512]{1,0:T(8,128)} %get-tuple-element.12), channel_id=1, source_target_pairs={{0,3},{32,35},{64,67},{96,99},{128,131},{160,163},{192,195},{224,2... | collective-permute-start | bytes 1572872 | tf_op jit(solution)/shard_map/ppermute | solution.py:275
  4.8 13.2 %collective-permute-start.2 = (f32[256,512]{1,0:T(8,128)S(1)}, f32[256,512]{1,0:T(8,128)}, u32[]{:S(2)}, u32[]{:S(2)}) collective-permute-start(f32[256,512]{1,0:T(8,128)S(1)} %get-tuple-element.13), channel_id=1, source_target_pairs={{0,1},{32,33},{64,65},{96,97},{128,129},{160,161},{192,193},{224,2... | collective-permute-start | bytes 1572872 | tf_op jit(solution)/shard_map/ppermute | solution.py:275
  6.2 11.7 %collective-permute-start = (f32[256,512]{1,0:T(8,128)S(1)}, f32[256,512]{1,0:T(8,128)}, u32[]{:S(2)}, u32[]{:S(2)}) collective-permute-start(f32[256,512]{1,0:T(8,128)S(1)} %get-tuple-element.13), channel_id=1, source_target_pairs={{0,32},{32,0},{1,33},{33,1},{2,34},{34,2},{3,35},{35,3},{4,36},{36... | collective-permute-start | bytes 1572872 | tf_op jit(solution)/shard_map/ppermute | solution.py:256
  9.2 27.0 %collective-permute-start.13 = (f32[512,512]{1,0:T(8,128)}, f32[512,512]{1,0:T(8,128)}, u32[]{:S(2)}, u32[]{:S(2)}) collective-permute-start(f32[512,512]{1,0:T(8,128)} %slice.40), channel_id=1, source_target_pairs={{0,256},{1,257},{2,258},{3,259},{4,260},{5,261},{6,262},{7,263},{8... | collective-permute-start | bytes 3145736 | tf_op jit(solution)/shard_map/ppermute | solution.py:296
  20.2 41.7 %copy-start.1 = (f32[256,512]{1,0:T(8,128)}, f32[256,512]{1,0:T(8,128)S(1)}, u32[]{:S(2)}) copy-start(f32[256,512]{1,0:T(8,128)S(1)} %get-tuple-element.9) | copy-start | bytes 1572868
  20.2 30.7 %all-to-all-start = ((f32[32,8,512]{2,1,0:T(8,128)}), f32[32,8,512]{2,1,0:T(8,128)S(1)}, u32[]{:S(2)}, u32[]{:S(2)}) async-start(f32[32,8,512]{2,1,0:T(8,128)} %get-tuple-element.10), calls=%async_computation | async-start | bytes 1048576 | tf_op jit(solution)/shard_map/all_to_all | solution.py:247
  37.3 38.2 %collective-permute-start.14 = (f32[512,512]{1,0:T(8,128)}, f32[512,512]{1,0:T(8,128)}, u32[]{:S(2)}, u32[]{:S(2)}) collective-permute-start(f32[512,512]{1,0:T(8,128)} %broadcast_select_fusion), channel_id=1, source_target_pairs={{0,128},{256,384},{1,129},{257,385},{2,130},{258,386},{3,131},{259... | collective-permute-start | bytes 3145736 | tf_op jit(solution)/shard_map/ppermute | solution.py:296
  51.6 18.0 %all-to-all-start.1 = ((f32[8,8,512]{2,1,0:T(8,128)}), f32[8,8,512]{2,1,0:T(8,128)S(1)}, u32[]{:S(2)}, u32[]{:S(2)}) async-start(f32[8,8,512]{2,1,0:T(8,128)} %broadcast_in_dim.20), calls=%async_computation.1 | async-start | bytes 262144 | tf_op jit(solution)/shard_map/all_to_all | solution.py:252
  60.4 21.0 %collective-permute-start.6 = (f32[256,512]{1,0:T(8,128)S(1)}, f32[256,512]{1,0:T(8,128)}, u32[]{:S(2)}, u32[]{:S(2)}) collective-permute-start(f32[256,512]{1,0:T(8,128)S(1)} %get-tuple-element.9), channel_id=1, source_target_pairs={{0,20},{1,21},{2,22},{3,23},{32,52},{33,53},{34,54},{35,55},{64,84... | collective-permute-start | bytes 1572872 | tf_op jit(solution)/shard_map/ppermute | solution.py:278
  61.9 19.6 %collective-permute-start.5 = (f32[256,512]{1,0:T(8,128)S(1)}, f32[256,512]{1,0:T(8,128)}, u32[]{:S(2)}, u32[]{:S(2)}) collective-permute-start(f32[256,512]{1,0:T(8,128)S(1)} %get-tuple-element.9), channel_id=1, source_target_pairs={{0,12},{1,13},{2,14},{3,15},{32,44},{33,45},{34,46},{35,47},{64,76... | collective-permute-start | bytes 1572872 | tf_op jit(solution)/shard_map/ppermute | solution.py:278
  70.4 20.2 %all-to-all-start.2 = ((f32[32,8,512]{2,1,0:T(8,128)}), f32[32,8,512]{2,1,0:T(8,128)S(1)}, u32[]{:S(2)}, u32[]{:S(2)}) async-start(f32[32,8,512]{2,1,0:T(8,128)} %broadcast_in_dim.22), calls=%async_computation.2 | async-start | bytes 1048576 | tf_op jit(solution)/shard_map/all_to_all | solution.py:252
  75.5 6.0 %copy-start.2 = (f32[256,512]{1,0:T(8,128)S(1)}, f32[256,512]{1,0:T(8,128)}, u32[]{:S(2)}) copy-start(f32[256,512]{1,0:T(8,128)} %copy-done.1) | copy-start | bytes 1572868
  78.0 21.4 %collective-permute-start.15 = (f32[512,512]{1,0:T(8,128)}, f32[512,512]{1,0:T(8,128)}, u32[]{:S(2)}, u32[]{:S(2)}) collective-permute-start(f32[512,512]{1,0:T(8,128)} %broadcast_select_fusion.1), channel_id=1, source_target_pairs={{0,64},{128,192},{256,320},{384,448},{1,65},{129,193},{257,321},{3... | collective-permute-start | bytes 3145736 | tf_op jit(solution)/shard_map/ppermute | solution.py:296
  82.8 9.6 %collective-permute-start.8 = (f32[256,512]{1,0:T(8,128)S(1)}, f32[256,512]{1,0:T(8,128)}, u32[]{:S(2)}, u32[]{:S(2)}) collective-permute-start(f32[256,512]{1,0:T(8,128)S(1)} %add_select_fusion.1), channel_id=1, source_target_pairs={{0,28},{12,8},{1,29},{13,9},{2,30},{14,10},{3,31},{15,11},{32,60},... | collective-permute-start | bytes 1572872 | tf_op jit(solution)/shard_map/ppermute | solution.py:281
  84.3 13.7 %collective-permute-start.7 = (f32[256,512]{1,0:T(8,128)S(1)}, f32[256,512]{1,0:T(8,128)}, u32[]{:S(2)}, u32[]{:S(2)}) collective-permute-start(f32[256,512]{1,0:T(8,128)S(1)} %add_select_fusion.1), channel_id=1, source_target_pairs={{0,4},{12,16},{20,24},{1,5},{13,17},{21,25},{2,6},{14,18},{22,26},... | collective-permute-start | bytes 1572872 | tf_op jit(solution)/shard_map/ppermute | solution.py:280
  90.6 11.6 %collective-permute-start.1 = (f32[256,512]{1,0:T(8,128)S(1)}, f32[256,512]{1,0:T(8,128)S(1)}, u32[]{:S(2)}, u32[]{:S(2)}) collective-permute-start(f32[256,512]{1,0:T(8,128)S(1)} %bitcast.11), channel_id=1, source_target_pairs={{0,32},{32,0},{1,33},{33,1},{2,34},{34,2},{3,35},{35,3},{4,36},{36... | collective-permute-start | bytes 1572872 | tf_op jit(solution)/shard_map/ppermute | solution.py:256
  100.8 36.4 %collective-permute-start.16 = (f32[512,512]{1,0:T(8,128)S(1)}, f32[512,512]{1,0:T(8,128)S(1)}, u32[]{:S(2)}, u32[]{:S(2)}) collective-permute-start(f32[512,512]{1,0:T(8,128)S(1)} %broadcast_select_fusion.2), channel_id=1, source_target_pairs={{0,32},{1,33},{2,34},{3,35},{4,36},{5,37},{6,38},{7,39},{8,40},{9,... | collective-permute-start | bytes 3145736 | tf_op jit(solution)/shard_map/ppermute | solution.py:298
  113.9 16.2 %collective-permute-start.11 = (f32[256,512]{1,0:T(8,128)S(1)}, f32[256,512]{1,0:T(8,128)S(1)}, u32[]{:S(2)}, u32[]{:S(2)}) collective-permute-start(f32[256,512]{1,0:T(8,128)S(1)} %get-tuple-element.7.own_ref), channel_id=1, source_target_pairs={{1,0},{2,1},{3,2},{0,3},{5,4},{6,5},{7,6},{4,7},{9,8},{10,9},{11,1... | collective-permute-start | bytes 1572872 | tf_op jit(solution)/shard_map/ppermute | solution.py:289
  118.2 17.1 %collective-permute-start.9 = (f32[256,512]{1,0:T(8,128)S(1)}, f32[256,512]{1,0:T(8,128)S(1)}, u32[]{:S(2)}, u32[]{:S(2)}) collective-permute-start(f32[256,512]{1,0:T(8,128)S(1)} %get-tuple-element.7.own_ref), channel_id=1, source_target_pairs={{0,1},{1,2},{2,3},{3,0},{4,5},{5,6},{6,7},{7,4},{8,9},{9,10},{10,1... | collective-permute-start | bytes 1572872 | tf_op jit(solution)/shard_map/ppermute | solution.py:288
  130.1 9.0 %collective-permute-start.12 = (f32[128,512]{1,0:T(8,128)S(1)}, f32[128,512]{1,0:T(8,128)S(1)}, u32[]{:S(2)}, u32[]{:S(2)}) collective-permute-start(f32[128,512]{1,0:T(8,128)S(1)} %slice.44), channel_id=1, source_target_pairs={{1,0},{2,1},{3,2},{0,3},{5,4},{6,5},{7,6},{4,7},{9,8},{10,9},{11,1... | collective-permute-start | bytes 786440 | tf_op jit(solution)/shard_map/ppermute | solution.py:291
  135.3 9.5 %collective-permute-start.10 = (f32[128,512]{1,0:T(8,128)S(1)}, f32[128,512]{1,0:T(8,128)S(1)}, u32[]{:S(2)}, u32[]{:S(2)}) collective-permute-start(f32[128,512]{1,0:T(8,128)S(1)} %slice.43), channel_id=1, source_target_pairs={{0,1},{1,2},{2,3},{3,0},{4,5},{5,6},{6,7},{7,4},{8,9},{9,10},{10,1... | collective-permute-start | bytes 786440 | tf_op jit(solution)/shard_map/ppermute | solution.py:290

commit v2 on v1

--- a/solution.py
+++ b/solution.py
@@ -96,66 +96,49 @@
         v_ref[there, :] -= _dot(v_ref[here, there].T, v_ref[here, :])
 
 
-def _first_kernel(here_ref, mine_ref, other_ref, v_ref):
-    half = NB // 2
-
-    @pl.when(here_ref[2] == 0)
-    def _():
-        v_ref[:half, :] = mine_ref[...]
-        v_ref[half:, :] = other_ref[...]
-
-    @pl.when(here_ref[2] != 0)
-    def _():
-        v_ref[:half, :] = other_ref[...]
-        v_ref[half:, :] = mine_ref[...]
-
-    _eliminate(0, v_ref)
-
-
-def _next_kernel(k, old_ref, v_ref):
+def _factor_kernel(k, old_ref, v_ref):
     v_ref[...] = old_ref[...]
     _eliminate(k, v_ref)
 
 
-def _handing_kernel(old_ref, _, v_ref, __):
-    _next_kernel(1, old_ref, v_ref)
-
-
-def factor_inverse(here, mine, other, own):
-    vmem = pl.BlockSpec(memory_space=pltpu.VMEM)
-    rest = dict(
-        out_shape=jax.ShapeDtypeStruct((NB, NB), jnp.float32),
-        out_specs=vmem,
-        compiler_params=pltpu.CompilerParams(vmem_limit_bytes=24 * 2**20),
-        cost_estimate=pl.CostEstimate(
-            flops=8 * 10**9, bytes_accessed=8 * NB * NB, transcendentals=NB
-        ),
-    )
-    state = pl.pallas_call(
-        _first_kernel,
-        in_specs=[pl.BlockSpec(memory_space=pltpu.SMEM), vmem, vmem],
-        name="factor_0",
-        **rest,
-    )(here, mine, other)
-    handed = dict(
-        rest,
-        out_shape=(rest["out_shape"], jax.ShapeDtypeStruct(own.shape, own.dtype)),
-        out_specs=(vmem, pl.BlockSpec(memory_space=pl.ANY)),
-        input_output_aliases={1: 1},
-    )
-    for k in range(1, NB // BK):
-        if k == 1:
-            state, own = pl.pallas_call(
-                _handing_kernel,
-                in_specs=[vmem, pl.BlockSpec(memory_space=pl.ANY)],
-                name="factor_1",
-                **handed,
-            )(state, own)
-        else:
-            state = pl.pallas_call(
-                functools.partial(_next_kernel, k), in_specs=[vmem], name=f"factor_{k}", **rest
-            )(state)
-    return state, own
+def factor_inverse(covariance):
+    state = covariance
+    for k in range(NB // BK):
+        state = pl.pallas_call(
+            functools.partial(_factor_kernel, k),
+            grid=(1,),
+            out_shape=jax.ShapeDtypeStruct((NB, NB), jnp.float32),
+            in_specs=[pl.BlockSpec((NB, NB), lambda i: (0, 0))],
+            out_specs=pl.BlockSpec((NB, NB), lambda i: (0, 0)),
+            compiler_params=pltpu.CompilerParams(vmem_limit_bytes=24 * 2**20),
+            cost_estimate=pl.CostEstimate(flops=10**6, bytes_accessed=10**5, transcendentals=NB),
+            name=f"factor_{k}",
+        )(state)
+    return state
+
+
+def _pick_kernel(which_ref, first_ref, *refs):
+    *others, o_ref, sem = refs
+    for i, ref in enumerate((first_ref.at[: o_ref.shape[0]], *others)):
+
+        @pl.when(which_ref[0] == i)
+        def _():
+            copy = pltpu.make_async_copy(ref, o_ref, sem)
+            copy.start()
+            copy.wait()
+
+
+def pick(which, first, *others):
+    return pl.pallas_call(
+        _pick_kernel,
+        out_shape=jax.ShapeDtypeStruct(others[0].shape, jnp.float32),
+        in_specs=[pl.BlockSpec(memory_space=pltpu.SMEM)]
+        + [pl.BlockSpec(memory_space=pl.ANY)] * (1 + len(others)),
+        out_specs=pl.BlockSpec(memory_space=pltpu.VMEM),
+        scratch_shapes=[pltpu.SemaphoreType.DMA],
+        cost_estimate=pl.CostEstimate(flops=0, bytes_accessed=10**6, transcendentals=0),
+        name="pick",
+    )(which.reshape(1), first, *others)
 
 
 def _split(value):
@@ -171,25 +154,38 @@
 
 
 def _update_kernel(
-    here_ref, state_ref, own_ref, back_ref, top_ref, low_ref, ahead_ref, tile_ref, inverse_ref,
-    o_ref, panel_ref, inv_ref, mirror_ref,
+    here_ref, state_ref, own_ref, back_ref, top_ref, low_ref, ahead_ref, tile_ref, sent_ref,
+    mine_ref, other_ref, o_ref, panel_ref, whole_ref, inv_ref, mirror_ref, sem,
 ):
-    row, col, x = here_ref[0], here_ref[1], here_ref[3]
+    row, col, core, x = (here_ref[j] for j in range(4))
     i = pl.program_id(0)
     first = pl.multiple_of(i * CHUNK, CHUNK)
     half = CHUNK // 2
 
     @pl.when(i == 0)
     def _():
-        for k in range(NB // BK):
-            here = slice(k * BK, (k + 1) * BK)
-            wide = inverse_ref[here, :]
-            lane = lax.broadcasted_iota(jnp.int32, wide.shape, 1)
-            top, low = _split(jnp.where(lane < (k + 1) * BK, wide, 0.0))
-            inv_ref[0, here, :] = top
-            inv_ref[1, here, :] = low
-
-        mirror = _split(_dot3((inv_ref[0], inv_ref[1]), _split(tile_ref[...]), ((1,), (0,))))
+        for value, ref in ((0, tile_ref), (1, sent_ref)):
+
+            @pl.when(core == value)
+            def _():
+                copy = pltpu.make_async_copy(ref, whole_ref, sem)
+                copy.start()
+                copy.wait()
+
+        tile = _split(whole_ref[...])
+        for value, parts in ((0, (mine_ref, other_ref)), (1, (other_ref, mine_ref))):
+
+            @pl.when(core == value)
+            def _():
+                for k in range(NB // BK):
+                    here = slice(k * BK, (k + 1) * BK)
+                    wide = parts[k // 2][(k % 2) * BK : (k % 2 + 1) * BK, :]
+                    lane = lax.broadcasted_iota(jnp.int32, wide.shape, 1)
+                    top, low = _split(jnp.where(lane < (k + 1) * BK, wide, 0.0))
+                    inv_ref[0, here, :] = top
+                    inv_ref[1, here, :] = low
+
+        mirror = _split(_dot3((inv_ref[0], inv_ref[1]), tile, ((1,), (0,))))
         mirror_ref[0] = mirror[0]
         mirror_ref[1] = mirror[1]
 
@@ -223,23 +219,29 @@
 def update(here, state, panel, mirror, inverse):
     block = pl.BlockSpec((CHUNK, NB), lambda i: (i, 0))
     vmem = pl.BlockSpec(memory_space=pltpu.VMEM)
+    anywhere = pl.BlockSpec(memory_space=pl.ANY)
     return pl.pallas_call(
         _update_kernel,
         grid=(state.shape[0] // CHUNK,),
         out_shape=jax.ShapeDtypeStruct(state.shape, jnp.float32),
-        in_specs=[pl.BlockSpec(memory_space=pltpu.SMEM), block] + [vmem] * 7,
+        in_specs=[pl.BlockSpec(memory_space=pltpu.SMEM), block]
+        + [vmem] * 5
+        + [anywhere] * 2
+        + [vmem] * 2,
         out_specs=block,
         scratch_shapes=[
             pltpu.VMEM((CHUNK, NB), jnp.float32),
+            pltpu.VMEM((NB, NB), jnp.float32),
             pltpu.VMEM((2, NB, NB), jnp.bfloat16),
             pltpu.VMEM((2, NB, NB), jnp.bfloat16),
+            pltpu.SemaphoreType.DMA,
         ],
         compiler_params=pltpu.CompilerParams(vmem_limit_bytes=40 * 2**20),
         cost_estimate=pl.CostEstimate(
             flops=30 * NB**3, bytes_accessed=32 * NB * NB, transcendentals=0
         ),
         name="update",
-    )(here, state, *panel, mirror, inverse)
+    )(here, state, *panel, *mirror, *inverse)
 
 
 def send_parts(value, axis, parts):
@@ -262,40 +264,33 @@
     half = NB // 2
     here = jnp.stack([y * 2 + core, z * nx + x, core, x]).astype(jnp.int32)
 
-    tile = covariance[:NB]
-    mine = jnp.where(core == 0, tile[:half], swap_cores(tile[half:]))
-
+    inverse = factor_inverse(covariance)
+    mine = pick(core, inverse, swap_cores(inverse[half:]))
     part = send_parts(mine, ("z", "x"), nz * nx)
     part = gather(part, "y", ny)[: part.shape[0]]
-    diagonal = gather(part, ("z", "x"), nz * nx)
-
-    size = covariance.shape[0] // nx
-    quarter = jnp.where(x == 0, covariance[:size], 0.0)
-    for i in range(1, nx):
-        quarter = quarter + lax.ppermute(
-            covariance[i * size : (i + 1) * size], ("z", "x"), [(0, i)]
-        )
+    mine = gather(part, ("z", "x"), nz * nx)
+    inverse = mine, swap_cores(mine)
+
+    quarter = send_parts(covariance, "x", nx)
     spread = lax.ppermute(quarter, "z", [(0, 3)]) + lax.ppermute(quarter, "z", [(0, 5)])
     spread = jnp.where(z == 0, quarter, spread)
     own = lax.ppermute(spread, "z", [(0, 1), (3, 4), (5, 6)])
     own = own + lax.ppermute(spread, "z", [(0, 7), (3, 2)])
     own = jnp.where((z == 0) | (z == 3) | (z == 5), spread, own)
-
-    inverse, own = factor_inverse(here, diagonal, swap_cores(diagonal), own)
-
     ring = [(i, (i + 1) % nx) for i in range(nx)]
     back_ring = [(j, i) for i, j in ring]
     back = lax.ppermute(own, "x", ring)
     ahead = lax.ppermute(own, "x", back_ring)
-    top = lax.ppermute(back[: size // 2], "x", ring)
-    low = lax.ppermute(ahead[size // 2 :], "x", back_ring)
-
-    mirror = tile
+    rest = own.shape[0] // 2
+    top = lax.ppermute(back[:rest], "x", ring)
+    low = lax.ppermute(ahead[rest:], "x", back_ring)
+
+    mirror = covariance[:NB]
     for step in (4, 2, 1):
         pairs = [(2 * i, 2 * (i + step)) for i in range(0, ny, 2 * step)]
         sent = lax.ppermute(mirror, ("y", "core"), pairs)
         mirror = jnp.where(y % (2 * step) == step, sent, mirror)
-    mirror = jnp.where(core == 0, mirror, lax.ppermute(mirror, "core", [(0, 1)]))
+    mirror = mirror, lax.ppermute(mirror, "core", [(0, 1)])
     return update(here, covariance, (own, back, top, low, ahead), mirror, inverse)
 
 

time: 153 us -> 150 us (0.980)
  waiting for transfers between devices: 31.9 us -> 25.4 us
  Pallas kernels: 28.8 us -> 32.3 us
  local copies, waits for them, and re-layouts: 5.2 us -> 8.46 us
  other arithmetic: 10.4 us -> 7.63 us
    ppermute x1, waiting for transfers between devices: 5.53 us -> 0.01 us  [body(): own = lax.ppermute(spread, 'z', [(0, 1), (3, 4), (5, 6)])]
    all_to_all x2, starting transfers between devices: 14 us -> 19.2 us  [gather(): return lax.all_to_all(copies, axis, 0, 0).reshape(-1, value.shape[1])]
    ppermute x3, starting transfers between devices: 17.7 us -> 13.3 us  [body(): sent = lax.ppermute(mirror, ('y', 'core'), pairs)]
    all_to_all x2, waiting for transfers between devices: 11 us -> 6.7 us  [gather(): return lax.all_to_all(copies, axis, 0, 0).reshape(-1, value.shape[1])]
    pallas_call x4 -> x5, Pallas kernels: 21.4 us -> 23.8 us  [the longest x4 22 us: factor_inverse(): pl.pallas_call(functools.partial(_factor_kernel, k), grid=(1,), out_shape...]
    add x1 -> x0, other arithmetic: 2.3 us -> none  [body(): quarter + lax.ppermute(covariance[i * size:(i + 1) * size], ('z', 'x'), [...]
    ppermute x6 -> x3, starting transfers between devices: 12 us -> 9.79 us  [the longest x1 5.59 us: body(): low = lax.ppermute(ahead[rest:], 'x', back_ring)]
    all_to_all x1 -> x2, waiting for transfers between devices: 8.06 us -> 9.86 us  [send_parts(): lax.all_to_all(value.reshape(parts, size, value.shape[1]), axis, 0, 0)[0]]
  transfers between devices with their start and end apart: 20 -> 18, of which waited for: 6 -> 6; matrix products, arithmetic and copies ran while one was open for 9% -> 9% of each run, Pallas kernels for 14% -> 16%
where the time goes in v2:
time: 150 us; the launch traced here: 149 us
  starting transfers between devices  75 us (50%)
  Pallas kernels  32.3 us (22%)
  waiting for transfers between devices  25.4 us (17%)
  local copies, waits for them, and re-layouts  8.46 us (6%)
  other arithmetic  7.63 us (5%)
    pallas_call x4, Pallas kernels, factor_inverse(): pl.pallas_call(functools.partial(_factor_kernel, k), grid=(1,), out_shape...  22 us
    all_to_all x2, starting transfers between devices, gather(): return lax.all_to_all(copies, axis, 0, 0).reshape(-1, value.shape[1])  19.2 us
    all_to_all x2, starting transfers between devices, send_parts(): lax.all_to_all(value.reshape(parts, size, value.shape[1]), axis, 0, 0)[0]  17.4 us
    ppermute x3, starting transfers between devices, body(): sent = lax.ppermute(mirror, ('y', 'core'), pairs)  13.3 us
    all_to_all x2, waiting for transfers between devices, send_parts(): lax.all_to_all(value.reshape(parts, size, value.shape[1]), axis, 0, 0)[0]  9.86 us
    pallas_call x1, Pallas kernels, update(): pl.pallas_call(_update_kernel, grid=(state.shape[0] // CHUNK,), out_shape...  8.5 us
    all_to_all x2, waiting for transfers between devices, gather(): return lax.all_to_all(copies, axis, 0, 0).reshape(-1, value.shape[1])  6.7 us
    ppermute x1, waiting for transfers between devices, body(): top = lax.ppermute(back[:rest], 'x', ring)  6.33 us
  transfers between devices with their start and end apart: 18, of which 6 were waited for; matrix products, arithmetic and copies ran while one was open for 9% of the time, Pallas kernels for 16%

profile of v2, /device:TPU:64, one launch (start us, length us, event | category | flops | bytes accessed | tf_op | source)
XLA Modules:
  0.0 149.2 jit_solution(6167898560338801245)
XLA Ops:
  0.0 2.3 %slice.25 = f32[512,512]{1,0:T(8,128)} slice(f32[1024,512]{1,0:T(8,128)} %state_ref.1), slice={[0:512], [0:512]} | slice | bytes 2097152 | tf_op jit(solution)/shard_map/slice | solution.py:288
  2.3 8.7 %collective-permute-start.8 = (f32[512,512]{1,0:T(8,128)}, f32[512,512]{1,0:T(8,128)}, u32[]{:S(2)}, u32[]{:S(2)}) collective-permute-start(f32[512,512]{1,0:T(8,128)} %slice.25), channel_id=1, source_target_pairs={{0,256},{1,257},{2,258},{3,259},{4,260},{5,261},{6,262},{7,263},{8... | collective-permute-start | bytes 3145736 | tf_op jit(solution)/shard_map/ppermute | solution.py:291
  11.0 4.3 %all-to-all-start = ((f32[4,256,512]{2,1,0:T(8,128)}), f32[4,256,512]{2,1,0:T(8,128)S(1)}, u32[]{:S(2)}, u32[]{:S(2)}) async-start(f32[4,256,512]{2,1,0:T(8,128)} %bitcast.4), calls=%async_computation | async-start | bytes 4194304 | tf_op jit(solution)/shard_map/all_to_all | solution.py:249
  15.3 6.8 %factor_0.1.old_ref = f32[512,512]{1,0:T(8,128)S(1)} custom-call(f32[1024,512]{1,0:T(8,128)} %state_ref.1), custom_call_target="tpu_custom_call" | custom-call | flops 1000000 | bytes 100000 | tf_op jit(solution)/shard_map/factor_0/pallas_call | solution.py:107
  22.1 5.3 %factor_1.1.old_ref = f32[512,512]{1,0:T(8,128)S(1)} custom-call(f32[512,512]{1,0:T(8,128)S(1)} %factor_0.1.old_ref), custom_call_target="tpu_custom_call" | custom-call | flops 1000000 | bytes 100000 | tf_op jit(solution)/shard_map/factor_1/pallas_call | solution.py:107
  27.4 5.0 %factor_2.1.old_ref = f32[512,512]{1,0:T(8,128)S(1)} custom-call(f32[512,512]{1,0:T(8,128)S(1)} %factor_1.1.old_ref), custom_call_target="tpu_custom_call" | custom-call | flops 1000000 | bytes 100000 | tf_op jit(solution)/shard_map/factor_2/pallas_call | solution.py:107
  32.4 4.9 %factor_3.1.first_ref = f32[512,512]{1,0:T(8,128)S(1)} custom-call(f32[512,512]{1,0:T(8,128)S(1)} %factor_2.1.old_ref), custom_call_target="tpu_custom_call" | custom-call | flops 1000000 | bytes 100000 | tf_op jit(solution)/shard_map/factor_3/pallas_call | solution.py:107
  37.3 0.9 slice.32
  38.2 1.9 %collective-permute-start.12 = (f32[256,512]{1,0:T(8,128)}, f32[256,512]{1,0:T(8,128)}, u32[]{:S(2)}, u32[]{:S(2)}) collective-permute-start(f32[256,512]{1,0:T(8,128)} %slice.32), channel_id=1, source_target_pairs={{0,32},{32,0},{1,33},{33,1},{2,34},{34,2},{3,35},{35,3},{4,36},{36... | collective-permute-start | bytes 1572872 | tf_op jit(solution)/shard_map/ppermute | solution.py:258
  40.1 0.0 collective-permute-done.8
  40.1 2.4 %broadcast_select_fusion = f32[512,512]{1,0:T(8,128)} fusion(f32[512,512]{1,0:T(8,128)} %collective-permute-done.8, pred[]{:T(512)S(6)} %eq.28, f32[1024,512]{1,0:T(8,128)} %state_ref.1), kind=kLoop, calls=%fused_computation.3 | loop fusion | flops 262144 | bytes 3145729 | tf_op jit(solution)/shard_map/jit(_where)/select_n | solution.py:292
  42.5 2.3 %collective-permute-start.9 = (f32[512,512]{1,0:T(8,128)}, f32[512,512]{1,0:T(8,128)}, u32[]{:S(2)}, u32[]{:S(2)}) collective-permute-start(f32[512,512]{1,0:T(8,128)} %broadcast_select_fusion), channel_id=1, source_target_pairs={{0,128},{256,384},{1,129},{257,385},{2,130},{258,386},{3,131},{259... | collective-permute-start | bytes 3145736 | tf_op jit(solution)/shard_map/ppermute | solution.py:291
  44.8 1.8 %pick.1 = f32[256,512]{1,0:T(8,128)} custom-call(s32[1]{0:T(128)} %bitcast.2.which_ref, f32[512,512]{1,0:T(8,128)} %copy-done, f32[256,512]{1,0:T(8,128)} %collective-permute-done.12.refs_0_), custom_call_target="tpu_custom_call" | custom-call | bytes 1000000 | tf_op jit(solution)/shard_map/pick/pallas_call | solution.py:132
  46.7 0.0 all-to-all-done
  46.7 13.2 %all-to-all-start.1 = ((f32[32,8,512]{2,1,0:T(8,128)}), f32[32,8,512]{2,1,0:T(8,128)}, u32[]{:S(2)}, u32[]{:S(2)}) async-start(f32[32,8,512]{2,1,0:T(8,128)} %bitcast.17), calls=%async_computation.1 | async-start | bytes 1048576 | tf_op jit(solution)/shard_map/all_to_all | solution.py:249
  59.8 0.8 slice_bitcast_fusion
  60.7 1.4 collective-permute-start.1
  62.1 1.5 collective-permute-start
  63.6 0.0 collective-permute-done.9
  63.6 1.4 broadcast_select_fusion.1
  65.0 2.3 %collective-permute-start.10 = (f32[512,512]{1,0:T(8,128)S(1)}, f32[512,512]{1,0:T(8,128)}, u32[]{:S(2)}, u32[]{:S(2)}) collective-permute-start(f32[512,512]{1,0:T(8,128)S(1)} %broadcast_select_fusion.1), channel_id=1, source_target_pairs={{0,64},{128,192},{256,320},{384,448},{1,65},{129,193},{257,321},{3... | collective-permute-start | bytes 3145736 | tf_op jit(solution)/shard_map/ppermute | solution.py:291
  67.3 9.9 %all-to-all-done.1 = f32[32,8,512]{2,1,0:T(8,128)} async-done(((f32[32,8,512]{2,1,0:T(8,128)}), f32[32,8,512]{2,1,0:T(8,128)}, u32[]{:S(2)}, u32[]{:S(2)}) %all-to-all-start.1) | async-done | bytes 524320 | tf_op jit(solution)/shard_map/all_to_all | solution.py:249
  77.2 0.7 slice_bitcast_fusion.2
  77.9 0.7 broadcast_in_dim.16
  78.6 3.4 %all-to-all-start.2 = ((f32[8,8,512]{2,1,0:T(8,128)}), f32[8,8,512]{2,1,0:T(8,128)S(1)}, u32[]{:S(2)}, u32[]{:S(2)}) async-start(f32[8,8,512]{2,1,0:T(8,128)} %broadcast_in_dim.16), calls=%async_computation.2 | async-start | bytes 262144 | tf_op jit(solution)/shard_map/all_to_all | solution.py:254
  82.0 2.1 %add_select_fusion.1 = f32[256,512]{1,0:T(8,128)} fusion(f32[256,512]{1,0:T(8,128)} %collective-permute-done, f32[256,512]{1,0:T(8,128)} %collective-permute-done.1, pred[]{:T(512)S(6)} %eq.23, f32[4,256,512]{2,1,0:T(8,128)S(1)} %all-to-all-done), kind=kLoop, calls=%fused_computation.2 | loop fusion | flops 262144 | bytes 2097153 | tf_op jit(solution)/shard_map/jit(_where)/select_n | solution.py:276
  84.1 0.7 collective-permute-start.3
  84.8 1.3 collective-permute-start.2
  86.1 4.8 %all-to-all-done.2 = f32[8,8,512]{2,1,0:T(8,128)S(1)} async-done(((f32[8,8,512]{2,1,0:T(8,128)}), f32[8,8,512]{2,1,0:T(8,128)S(1)}, u32[]{:S(2)}, u32[]{:S(2)}) %all-to-all-start.2) | async-done | bytes 131104 | tf_op jit(solution)/shard_map/all_to_all | solution.py:254
  90.9 0.9 broadcast_in_dim.18
  91.8 15.8 %all-to-all-start.3 = ((f32[32,8,512]{2,1,0:T(8,128)}), f32[32,8,512]{2,1,0:T(8,128)S(1)}, u32[]{:S(2)}, u32[]{:S(2)}) async-start(f32[32,8,512]{2,1,0:T(8,128)} %broadcast_in_dim.18), calls=%async_computation.3 | async-start | bytes 1048576 | tf_op jit(solution)/shard_map/all_to_all | solution.py:254
  107.7 0.2 broadcast_select_fusion.2.tile_ref
  107.9 2.3 %collective-permute-start.11 = (f32[512,512]{1,0:T(8,128)S(1)}, f32[512,512]{1,0:T(8,128)}, u32[]{:S(2)}, u32[]{:S(2)}) collective-permute-start(f32[512,512]{1,0:T(8,128)S(1)} %broadcast_select_fusion.2.tile_ref), channel_id=1, source_target_pairs={{0,32},{1,33},{2,34},{3,35},{4,36},{5,37},{6,38},{7,39},{8,40},{9,... | collective-permute-start | bytes 3145736 | tf_op jit(solution)/shard_map/ppermute | solution.py:293
  110.2 0.8 copy-done.1
  111.0 1.3 add_select_fusion.own_ref
  112.4 4.6 %collective-permute-start.6 = (f32[256,512]{1,0:T(8,128)S(1)}, f32[256,512]{1,0:T(8,128)S(1)}, u32[]{:S(2)}, u32[]{:S(2)}) collective-permute-start(f32[256,512]{1,0:T(8,128)S(1)} %add_select_fusion.own_ref), channel_id=1, source_target_pairs={{1,0},{2,1},{3,2},{0,3},{5,4},{6,5},{7,6},{4,7},{9,8},{10,9},{11,1... | collective-permute-start | bytes 1572872 | tf_op jit(solution)/shard_map/ppermute | solution.py:283
  116.9 1.9 %collective-permute-start.4 = (f32[256,512]{1,0:T(8,128)S(1)}, f32[256,512]{1,0:T(8,128)S(1)}, u32[]{:S(2)}, u32[]{:S(2)}) collective-permute-start(f32[256,512]{1,0:T(8,128)S(1)} %add_select_fusion.own_ref), channel_id=1, source_target_pairs={{0,1},{1,2},{2,3},{3,0},{4,5},{5,6},{6,7},{7,4},{8,9},{9,10},{10,1... | collective-permute-start | bytes 1572872 | tf_op jit(solution)/shard_map/ppermute | solution.py:282
  118.9 1.9 %all-to-all-done.3 = f32[32,8,512]{2,1,0:T(8,128)S(1)} async-done(((f32[32,8,512]{2,1,0:T(8,128)}), f32[32,8,512]{2,1,0:T(8,128)S(1)}, u32[]{:S(2)}, u32[]{:S(2)}) %all-to-all-start.3) | async-done | bytes 524320 | tf_op jit(solution)/shard_map/all_to_all | solution.py:254
  120.7 1.9 %collective-permute-start.13 = (f32[256,512]{1,0:T(8,128)S(1)}, f32[256,512]{1,0:T(8,128)}, u32[]{:S(2)}, u32[]{:S(2)}) collective-permute-start(f32[256,512]{1,0:T(8,128)S(1)} %bitcast.15), channel_id=1, source_target_pairs={{0,32},{32,0},{1,33},{33,1},{2,34},{34,2},{3,35},{35,3},{4,36},{36... | collective-permute-start | bytes 1572872 | tf_op jit(solution)/shard_map/ppermute | solution.py:258
  122.7 1.0 collective-permute-done.6.ahead_ref
  123.7 0.7 slice.31
  124.4 5.6 %collective-permute-start.7 = (f32[128,512]{1,0:T(8,128)}, f32[128,512]{1,0:T(8,128)S(1)}, u32[]{:S(2)}, u32[]{:S(2)}) collective-permute-start(f32[128,512]{1,0:T(8,128)} %slice.31), channel_id=1, source_target_pairs={{1,0},{2,1},{3,2},{0,3},{5,4},{6,5},{7,6},{4,7},{9,8},{10,9},{11,1... | collective-permute-start | bytes 786440 | tf_op jit(solution)/shard_map/ppermute | solution.py:286
  130.0 0.7 slice.30
  130.7 1.9 %collective-permute-start.5 = (f32[128,512]{1,0:T(8,128)}, f32[128,512]{1,0:T(8,128)}, u32[]{:S(2)}, u32[]{:S(2)}) collective-permute-start(f32[128,512]{1,0:T(8,128)} %slice.30), channel_id=1, source_target_pairs={{0,1},{1,2},{2,3},{3,0},{4,5},{5,6},{6,7},{7,4},{8,9},{9,10},{10,1... | collective-permute-start | bytes 786440 | tf_op jit(solution)/shard_map/ppermute | solution.py:285
  132.7 0.1 pad_add_fusion.here_ref
  132.8 1.4 collective-permute-done.7.low_ref
  134.2 6.3 %collective-permute-done.5.top_ref = f32[128,512]{1,0:T(8,128)} collective-permute-done((f32[128,512]{1,0:T(8,128)}, f32[128,512]{1,0:T(8,128)}, u32[]{:S(2)}, u32[]{:S(2)}) %collective-permute-start.5) | collective-permute-done | bytes 262176 | tf_op jit(solution)/shard_map/ppermute | solution.py:285
  140.5 8.5 %update.1 = f32[1024,512]{1,0:T(8,128)} custom-call(s32[4]{0:T(128)S(1)} %pad_add_fusion.here_ref, f32[1024,512]{1,0:T(8,128)} %state_ref.1, f32[256,512]{1,0:T(8,128)S(1)} %add_select_fusion.own_ref, f32[256,512]{1,0:T(8,128)S(1)} %collective-permute-done.4.back_ref, f32[128,512]{1,0:T(8,128)} %collective-permute-done.5.top_ref, ...), custom_call_target="tpu_custom_call" | custom-call | flops 4026531840 | bytes 8388608 | tf_op jit(solution)/shard_map/update/pallas_call | solution.py:223
  (13 shorter events, 0.0 us)
Async XLA Ops:
  2.3 37.8 %collective-permute-start.8 = (f32[512,512]{1,0:T(8,128)}, f32[512,512]{1,0:T(8,128)}, u32[]{:S(2)}, u32[]{:S(2)}) collective-permute-start(f32[512,512]{1,0:T(8,128)} %slice.25), channel_id=1, source_target_pairs={{0,256},{1,257},{2,258},{3,259},{4,260},{5,261},{6,262},{7,263},{8... | collective-permute-start | bytes 3145736 | tf_op jit(solution)/shard_map/ppermute | solution.py:291
  11.0 35.7 %all-to-all-start = ((f32[4,256,512]{2,1,0:T(8,128)}), f32[4,256,512]{2,1,0:T(8,128)S(1)}, u32[]{:S(2)}, u32[]{:S(2)}) async-start(f32[4,256,512]{2,1,0:T(8,128)} %bitcast.4), calls=%async_computation | async-start | bytes 4194304 | tf_op jit(solution)/shard_map/all_to_all | solution.py:249
  37.3 5.2 %copy-start = (f32[512,512]{1,0:T(8,128)}, f32[512,512]{1,0:T(8,128)S(1)}, u32[]{:S(2)}) copy-start(f32[512,512]{1,0:T(8,128)S(1)} %factor_3.1.first_ref) | copy-start | bytes 3145732
  38.2 6.6 %collective-permute-start.12 = (f32[256,512]{1,0:T(8,128)}, f32[256,512]{1,0:T(8,128)}, u32[]{:S(2)}, u32[]{:S(2)}) collective-permute-start(f32[256,512]{1,0:T(8,128)} %slice.32), channel_id=1, source_target_pairs={{0,32},{32,0},{1,33},{33,1},{2,34},{34,2},{3,35},{35,3},{4,36},{36... | collective-permute-start | bytes 1572872 | tf_op jit(solution)/shard_map/ppermute | solution.py:258
  42.5 21.1 %collective-permute-start.9 = (f32[512,512]{1,0:T(8,128)}, f32[512,512]{1,0:T(8,128)}, u32[]{:S(2)}, u32[]{:S(2)}) collective-permute-start(f32[512,512]{1,0:T(8,128)} %broadcast_select_fusion), channel_id=1, source_target_pairs={{0,128},{256,384},{1,129},{257,385},{2,130},{258,386},{3,131},{259... | collective-permute-start | bytes 3145736 | tf_op jit(solution)/shard_map/ppermute | solution.py:291
  46.7 30.5 %all-to-all-start.1 = ((f32[32,8,512]{2,1,0:T(8,128)}), f32[32,8,512]{2,1,0:T(8,128)}, u32[]{:S(2)}, u32[]{:S(2)}) async-start(f32[32,8,512]{2,1,0:T(8,128)} %bitcast.17), calls=%async_computation.1 | async-start | bytes 1048576 | tf_op jit(solution)/shard_map/all_to_all | solution.py:249
  60.7 21.3 %collective-permute-start.1 = (f32[256,512]{1,0:T(8,128)}, f32[256,512]{1,0:T(8,128)}, u32[]{:S(2)}, u32[]{:S(2)}) collective-permute-start(f32[256,512]{1,0:T(8,128)} %slice_bitcast_fusion), channel_id=1, source_target_pairs={{0,20},{1,21},{2,22},{3,23},{32,52},{33,53},{34,54},{35,55},{64,84... | collective-permute-start | bytes 1572872 | tf_op jit(solution)/shard_map/ppermute | solution.py:275
  62.1 19.8 %collective-permute-start = (f32[256,512]{1,0:T(8,128)}, f32[256,512]{1,0:T(8,128)}, u32[]{:S(2)}, u32[]{:S(2)}) collective-permute-start(f32[256,512]{1,0:T(8,128)} %slice_bitcast_fusion), channel_id=1, source_target_pairs={{0,12},{1,13},{2,14},{3,15},{32,44},{33,45},{34,46},{35,47},{64,76... | collective-permute-start | bytes 1572872 | tf_op jit(solution)/shard_map/ppermute | solution.py:275
  65.0 42.7 %collective-permute-start.10 = (f32[512,512]{1,0:T(8,128)S(1)}, f32[512,512]{1,0:T(8,128)}, u32[]{:S(2)}, u32[]{:S(2)}) collective-permute-start(f32[512,512]{1,0:T(8,128)S(1)} %broadcast_select_fusion.1), channel_id=1, source_target_pairs={{0,64},{128,192},{256,320},{384,448},{1,65},{129,193},{257,321},{3... | collective-permute-start | bytes 3145736 | tf_op jit(solution)/shard_map/ppermute | solution.py:291
  78.6 12.4 %all-to-all-start.2 = ((f32[8,8,512]{2,1,0:T(8,128)}), f32[8,8,512]{2,1,0:T(8,128)S(1)}, u32[]{:S(2)}, u32[]{:S(2)}) async-start(f32[8,8,512]{2,1,0:T(8,128)} %broadcast_in_dim.16), calls=%async_computation.2 | async-start | bytes 262144 | tf_op jit(solution)/shard_map/all_to_all | solution.py:254
  84.1 26.1 %collective-permute-start.3 = (f32[256,512]{1,0:T(8,128)}, f32[256,512]{1,0:T(8,128)S(1)}, u32[]{:S(2)}, u32[]{:S(2)}) collective-permute-start(f32[256,512]{1,0:T(8,128)} %add_select_fusion.1), channel_id=1, source_target_pairs={{0,28},{12,8},{1,29},{13,9},{2,30},{14,10},{3,31},{15,11},{32,60},... | collective-permute-start | bytes 1572872 | tf_op jit(solution)/shard_map/ppermute | solution.py:278
  84.8 26.2 %collective-permute-start.2 = (f32[256,512]{1,0:T(8,128)}, f32[256,512]{1,0:T(8,128)}, u32[]{:S(2)}, u32[]{:S(2)}) collective-permute-start(f32[256,512]{1,0:T(8,128)} %add_select_fusion.1), channel_id=1, source_target_pairs={{0,4},{12,16},{20,24},{1,5},{13,17},{21,25},{2,6},{14,18},{22,26},... | collective-permute-start | bytes 1572872 | tf_op jit(solution)/shard_map/ppermute | solution.py:277
  91.8 28.9 %all-to-all-start.3 = ((f32[32,8,512]{2,1,0:T(8,128)}), f32[32,8,512]{2,1,0:T(8,128)S(1)}, u32[]{:S(2)}, u32[]{:S(2)}) async-start(f32[32,8,512]{2,1,0:T(8,128)} %broadcast_in_dim.18), calls=%async_computation.3 | async-start | bytes 1048576 | tf_op jit(solution)/shard_map/all_to_all | solution.py:254
  107.9 32.6 %collective-permute-start.11 = (f32[512,512]{1,0:T(8,128)S(1)}, f32[512,512]{1,0:T(8,128)}, u32[]{:S(2)}, u32[]{:S(2)}) collective-permute-start(f32[512,512]{1,0:T(8,128)S(1)} %broadcast_select_fusion.2.tile_ref), channel_id=1, source_target_pairs={{0,32},{1,33},{2,34},{3,35},{4,36},{5,37},{6,38},{7,39},{8,40},{9,... | collective-permute-start | bytes 3145736 | tf_op jit(solution)/shard_map/ppermute | solution.py:293
  110.2 0.8 copy-start.1
  112.4 11.4 %collective-permute-start.6 = (f32[256,512]{1,0:T(8,128)S(1)}, f32[256,512]{1,0:T(8,128)S(1)}, u32[]{:S(2)}, u32[]{:S(2)}) collective-permute-start(f32[256,512]{1,0:T(8,128)S(1)} %add_select_fusion.own_ref), channel_id=1, source_target_pairs={{1,0},{2,1},{3,2},{0,3},{5,4},{6,5},{7,6},{4,7},{9,8},{10,9},{11,1... | collective-permute-start | bytes 1572872 | tf_op jit(solution)/shard_map/ppermute | solution.py:283
  116.9 13.1 %collective-permute-start.4 = (f32[256,512]{1,0:T(8,128)S(1)}, f32[256,512]{1,0:T(8,128)S(1)}, u32[]{:S(2)}, u32[]{:S(2)}) collective-permute-start(f32[256,512]{1,0:T(8,128)S(1)} %add_select_fusion.own_ref), channel_id=1, source_target_pairs={{0,1},{1,2},{2,3},{3,0},{4,5},{5,6},{6,7},{7,4},{8,9},{9,10},{10,1... | collective-permute-start | bytes 1572872 | tf_op jit(solution)/shard_map/ppermute | solution.py:282
  120.7 12.0 %collective-permute-start.13 = (f32[256,512]{1,0:T(8,128)S(1)}, f32[256,512]{1,0:T(8,128)}, u32[]{:S(2)}, u32[]{:S(2)}) collective-permute-start(f32[256,512]{1,0:T(8,128)S(1)} %bitcast.15), channel_id=1, source_target_pairs={{0,32},{32,0},{1,33},{33,1},{2,34},{34,2},{3,35},{35,3},{4,36},{36... | collective-permute-start | bytes 1572872 | tf_op jit(solution)/shard_map/ppermute | solution.py:258
  124.4 9.8 %collective-permute-start.7 = (f32[128,512]{1,0:T(8,128)}, f32[128,512]{1,0:T(8,128)S(1)}, u32[]{:S(2)}, u32[]{:S(2)}) collective-permute-start(f32[128,512]{1,0:T(8,128)} %slice.31), channel_id=1, source_target_pairs={{1,0},{2,1},{3,2},{0,3},{5,4},{6,5},{7,6},{4,7},{9,8},{10,9},{11,1... | collective-permute-start | bytes 786440 | tf_op jit(solution)/shard_map/ppermute | solution.py:286
  130.7 9.8 %collective-permute-start.5 = (f32[128,512]{1,0:T(8,128)}, f32[128,512]{1,0:T(8,128)}, u32[]{:S(2)}, u32[]{:S(2)}) collective-permute-start(f32[128,512]{1,0:T(8,128)} %slice.30), channel_id=1, source_target_pairs={{0,1},{1,2},{2,3},{3,0},{4,5},{5,6},{6,7},{7,4},{8,9},{9,10},{10,1... | collective-permute-start | bytes 786440 | tf_op jit(solution)/shard_map/ppermute | solution.py:285

commit v3 on v1

--- a/solution.py
+++ b/solution.py
@@ -117,19 +117,13 @@
     _eliminate(k, v_ref)
 
 
-def _handing_kernel(old_ref, _, v_ref, __):
-    _next_kernel(1, old_ref, v_ref)
-
-
-def factor_inverse(here, mine, other, own):
+def factor_inverse(here, mine, other):
     vmem = pl.BlockSpec(memory_space=pltpu.VMEM)
     rest = dict(
         out_shape=jax.ShapeDtypeStruct((NB, NB), jnp.float32),
         out_specs=vmem,
         compiler_params=pltpu.CompilerParams(vmem_limit_bytes=24 * 2**20),
-        cost_estimate=pl.CostEstimate(
-            flops=8 * 10**9, bytes_accessed=8 * NB * NB, transcendentals=NB
-        ),
+        cost_estimate=pl.CostEstimate(flops=10**6, bytes_accessed=10**5, transcendentals=NB),
     )
     state = pl.pallas_call(
         _first_kernel,
@@ -137,25 +131,35 @@
         name="factor_0",
         **rest,
     )(here, mine, other)
-    handed = dict(
-        rest,
-        out_shape=(rest["out_shape"], jax.ShapeDtypeStruct(own.shape, own.dtype)),
-        out_specs=(vmem, pl.BlockSpec(memory_space=pl.ANY)),
-        input_output_aliases={1: 1},
-    )
     for k in range(1, NB // BK):
-        if k == 1:
-            state, own = pl.pallas_call(
-                _handing_kernel,
-                in_specs=[vmem, pl.BlockSpec(memory_space=pl.ANY)],
-                name="factor_1",
-                **handed,
-            )(state, own)
-        else:
-            state = pl.pallas_call(
-                functools.partial(_next_kernel, k), in_specs=[vmem], name=f"factor_{k}", **rest
-            )(state)
-    return state, own
+        state = pl.pallas_call(
+            functools.partial(_next_kernel, k), in_specs=[vmem], name=f"factor_{k}", **rest
+        )(state)
+    return state
+
+
+def _pick_kernel(which_ref, first_ref, *refs):
+    *others, _, o_ref, sem = refs
+    for i, ref in enumerate((first_ref.at[: o_ref.shape[0]], *others)):
+
+        @pl.when(which_ref[0] == i)
+        def _():
+            copy = pltpu.make_async_copy(ref, o_ref, sem)
+            copy.start()
+            copy.wait()
+
+
+def pick(which, first, *others, after):
+    return pl.pallas_call(
+        _pick_kernel,
+        out_shape=jax.ShapeDtypeStruct(others[0].shape, jnp.float32),
+        in_specs=[pl.BlockSpec(memory_space=pltpu.SMEM)]
+        + [pl.BlockSpec(memory_space=pl.ANY)] * (2 + len(others)),
+        out_specs=pl.BlockSpec(memory_space=pltpu.VMEM),
+        scratch_shapes=[pltpu.SemaphoreType.DMA],
+        cost_estimate=pl.CostEstimate(flops=0, bytes_accessed=10**6, transcendentals=0),
+        name="pick",
+    )(which.reshape(1), first, *others, after)
 
 
 def _split(value):
@@ -171,16 +175,23 @@
 
 
 def _update_kernel(
-    here_ref, state_ref, own_ref, back_ref, top_ref, low_ref, ahead_ref, tile_ref, inverse_ref,
-    o_ref, panel_ref, inv_ref, mirror_ref,
+    here_ref, state_ref, panel_ref, tile_ref, sent_ref, inverse_ref,
+    o_ref, whole_ref, inv_ref, mirror_ref, sem,
 ):
-    row, col, x = here_ref[0], here_ref[1], here_ref[3]
+    row, col, core = (here_ref[j] for j in range(3))
     i = pl.program_id(0)
     first = pl.multiple_of(i * CHUNK, CHUNK)
-    half = CHUNK // 2
 
     @pl.when(i == 0)
     def _():
+        for value, ref in ((0, tile_ref), (1, sent_ref)):
+
+            @pl.when(core == value)
+            def _():
+                copy = pltpu.make_async_copy(ref, whole_ref, sem)
+                copy.start()
+                copy.wait()
+
         for k in range(NB // BK):
             here = slice(k * BK, (k + 1) * BK)
             wide = inverse_ref[here, :]
@@ -188,22 +199,9 @@
             top, low = _split(jnp.where(lane < (k + 1) * BK, wide, 0.0))
             inv_ref[0, here, :] = top
             inv_ref[1, here, :] = low
-
-        mirror = _split(_dot3((inv_ref[0], inv_ref[1]), _split(tile_ref[...]), ((1,), (0,))))
+        mirror = _split(_dot3((inv_ref[0], inv_ref[1]), _split(whole_ref[...]), ((1,), (0,))))
         mirror_ref[0] = mirror[0]
         mirror_ref[1] = mirror[1]
-
-    turn = lax.rem(x + 4 - i, 4)
-    for j, part in ((0, own_ref), (1, back_ref), (3, ahead_ref)):
-
-        @pl.when(turn == j)
-        def _():
-            panel_ref[...] = part[...]
-
-    @pl.when(turn == 2)
-    def _():
-        panel_ref[:half, :] = top_ref[...]
-        panel_ref[half:, :] = low_ref[...]
 
     solved = _dot3(_split(panel_ref[...]), (inv_ref[0], inv_ref[1]), ((1,), (1,)))
     top = (row == 0) & (first < NB)
@@ -222,24 +220,27 @@
 
 def update(here, state, panel, mirror, inverse):
     block = pl.BlockSpec((CHUNK, NB), lambda i: (i, 0))
-    vmem = pl.BlockSpec(memory_space=pltpu.VMEM)
+    tile = pl.BlockSpec((NB, NB), lambda i: (0, 0))
     return pl.pallas_call(
         _update_kernel,
         grid=(state.shape[0] // CHUNK,),
         out_shape=jax.ShapeDtypeStruct(state.shape, jnp.float32),
-        in_specs=[pl.BlockSpec(memory_space=pltpu.SMEM), block] + [vmem] * 7,
+        in_specs=[pl.BlockSpec(memory_space=pltpu.SMEM), block, block]
+        + [pl.BlockSpec(memory_space=pl.ANY)] * 2
+        + [tile],
         out_specs=block,
         scratch_shapes=[
-            pltpu.VMEM((CHUNK, NB), jnp.float32),
+            pltpu.VMEM((NB, NB), jnp.float32),
             pltpu.VMEM((2, NB, NB), jnp.bfloat16),
             pltpu.VMEM((2, NB, NB), jnp.bfloat16),
+            pltpu.SemaphoreType.DMA,
         ],
         compiler_params=pltpu.CompilerParams(vmem_limit_bytes=40 * 2**20),
         cost_estimate=pl.CostEstimate(
             flops=30 * NB**3, bytes_accessed=32 * NB * NB, transcendentals=0
         ),
         name="update",
-    )(here, state, *panel, mirror, inverse)
+    )(here, state, panel, *mirror, inverse)
 
 
 def send_parts(value, axis, parts):
@@ -260,43 +261,29 @@
     ny, nz, nx = (lax.axis_size(axis) for axis in ("y", "z", "x"))
     core, x, y, z = (lax.axis_index(axis) for axis in ("core", "x", "y", "z"))
     half = NB // 2
-    here = jnp.stack([y * 2 + core, z * nx + x, core, x]).astype(jnp.int32)
-
-    tile = covariance[:NB]
-    mine = jnp.where(core == 0, tile[:half], swap_cores(tile[half:]))
-
-    part = send_parts(mine, ("z", "x"), nz * nx)
-    part = gather(part, "y", ny)[: part.shape[0]]
-    diagonal = gather(part, ("z", "x"), nz * nx)
-
-    size = covariance.shape[0] // nx
-    quarter = jnp.where(x == 0, covariance[:size], 0.0)
-    for i in range(1, nx):
-        quarter = quarter + lax.ppermute(
-            covariance[i * size : (i + 1) * size], ("z", "x"), [(0, i)]
-        )
+    here = jnp.stack([y * 2 + core, z * nx + x, core]).astype(jnp.int32)
+
+    quarter = send_parts(covariance, "x", nx)
     spread = lax.ppermute(quarter, "z", [(0, 3)]) + lax.ppermute(quarter, "z", [(0, 5)])
     spread = jnp.where(z == 0, quarter, spread)
     own = lax.ppermute(spread, "z", [(0, 1), (3, 4), (5, 6)])
     own = own + lax.ppermute(spread, "z", [(0, 7), (3, 2)])
     own = jnp.where((z == 0) | (z == 3) | (z == 5), spread, own)
-
-    inverse, own = factor_inverse(here, diagonal, swap_cores(diagonal), own)
-
-    ring = [(i, (i + 1) % nx) for i in range(nx)]
-    back_ring = [(j, i) for i, j in ring]
-    back = lax.ppermute(own, "x", ring)
-    ahead = lax.ppermute(own, "x", back_ring)
-    top = lax.ppermute(back[: size // 2], "x", ring)
-    low = lax.ppermute(ahead[size // 2 :], "x", back_ring)
-
-    mirror = tile
+    panel = gather(own, "x", nx)
+
+    mine = pick(core, covariance, swap_cores(covariance[half:NB]), after=quarter)
+    part = send_parts(mine, ("z", "x"), nz * nx)
+    part = gather(part, "y", ny)[: part.shape[0]]
+    diagonal = gather(part, ("z", "x"), nz * nx)
+    inverse = factor_inverse(here, diagonal, swap_cores(diagonal))
+
+    mirror = covariance[:NB]
     for step in (4, 2, 1):
         pairs = [(2 * i, 2 * (i + step)) for i in range(0, ny, 2 * step)]
         sent = lax.ppermute(mirror, ("y", "core"), pairs)
         mirror = jnp.where(y % (2 * step) == step, sent, mirror)
-    mirror = jnp.where(core == 0, mirror, lax.ppermute(mirror, "core", [(0, 1)]))
-    return update(here, covariance, (own, back, top, low, ahead), mirror, inverse)
+    mirror = mirror, lax.ppermute(mirror, "core", [(0, 1)])
+    return update(here, covariance, panel, mirror, inverse)
 
 
 def solution(mesh):

time: 153 us -> 163 us (1.065)
  the two profiles are of different devices: /device:TPU:64 before, /device:TPU:131 now
where the time goes in v3:
time: 163 us; the launch traced here: 162 us
  starting transfers between devices  73.9 us (45%)
  waiting for transfers between devices  39.2 us (24%)
  Pallas kernels  32.6 us (20%)
  local copies, waits for them, and re-layouts  8.46 us (5%)
  other arithmetic  7.58 us (5%)
    ppermute x2, starting transfers between devices, swap_cores(): return lax.ppermute(value, 'core', [(0, 1), (1, 0)])  26.5 us
    all_to_all x2, waiting for transfers between devices, send_parts(): lax.all_to_all(value.reshape(parts, size, value.shape[1]), axis, 0, 0)[0]  20.6 us
    all_to_all x3, starting transfers between devices, gather(): return lax.all_to_all(copies, axis, 0, 0).reshape(-1, value.shape[1])  20.5 us
    pallas_call x3, Pallas kernels, factor_inverse(): pl.pallas_call(functools.partial(_next_kernel, k), in_specs=[vmem], name=...  15.2 us
    all_to_all x2, starting transfers between devices, send_parts(): lax.all_to_all(value.reshape(parts, size, value.shape[1]), axis, 0, 0)[0]  15 us
    ppermute x1, waiting for transfers between devices, body(): own = own + lax.ppermute(spread, 'z', [(0, 7), (3, 2)])  12 us
    pallas_call x1, Pallas kernels, update(): pl.pallas_call(_update_kernel, grid=(state.shape[0] // CHUNK,), out_shape...  9 us
    pallas_call x1, Pallas kernels, factor_inverse(): pl.pallas_call(_first_kernel, in_specs=[pl.BlockSpec(memory_space=pltpu.S...  6.41 us
  transfers between devices with their start and end apart: 15, of which 5 were waited for; matrix products, arithmetic and copies ran while one was open for 9% of the time, Pallas kernels for 15%

profile of v3, /device:TPU:131, one launch (start us, length us, event | category | flops | bytes accessed | tf_op | source)
XLA Modules:
  0.0 162.1 jit_solution(16868853066517377563)
XLA Ops:
  0.0 4.8 %all-to-all-start = ((f32[4,256,512]{2,1,0:T(8,128)}), f32[4,256,512]{2,1,0:T(8,128)}, u32[]{:S(2)}, u32[]{:S(2)}) async-start(f32[4,256,512]{2,1,0:T(8,128)} %bitcast.15), calls=%async_computation | async-start | bytes 4194304 | tf_op jit(solution)/shard_map/all_to_all | solution.py:248
  4.8 0.1 slice.17
  4.9 1.7 %collective-permute-start.4 = (f32[512,512]{1,0:T(8,128)S(1)}, f32[512,512]{1,0:T(8,128)}, u32[]{:S(2)}, u32[]{:S(2)}) collective-permute-start(f32[512,512]{1,0:T(8,128)S(1)} %slice.17), channel_id=1, source_target_pairs={{0,256},{1,257},{2,258},{3,259},{4,260},{5,261},{6,262},{7,263},{8... | collective-permute-start | bytes 3145736 | tf_op jit(solution)/shard_map/ppermute | solution.py:283
  6.5 0.8 slice.18
  7.4 9.9 %collective-permute-start.8 = (f32[256,512]{1,0:T(8,128)}, f32[256,512]{1,0:T(8,128)S(1)}, u32[]{:S(2)}, u32[]{:S(2)}) collective-permute-start(f32[256,512]{1,0:T(8,128)} %slice.18), channel_id=1, source_target_pairs={{0,32},{32,0},{1,33},{33,1},{2,34},{34,2},{3,35},{35,3},{4,36},{36... | collective-permute-start | bytes 1572872 | tf_op jit(solution)/shard_map/ppermute | solution.py:257
  17.3 12.2 %all-to-all-done = f32[4,256,512]{2,1,0:T(8,128)} async-done(((f32[4,256,512]{2,1,0:T(8,128)}), f32[4,256,512]{2,1,0:T(8,128)}, u32[]{:S(2)}, u32[]{:S(2)}) %all-to-all-start) | async-done | bytes 2097184 | tf_op jit(solution)/shard_map/all_to_all | solution.py:248
  29.5 1.9 %slice_bitcast_fusion.refs_1_ = f32[256,512]{1,0:T(8,128)} fusion(f32[4,256,512]{2,1,0:T(8,128)} %all-to-all-done), kind=kLoop, calls=%fused_computation | loop fusion | bytes 1048576 | tf_op jit(solution)/shard_map/squeeze | solution.py:248
  31.3 0.0 collective-permute-done.8.refs_0_
  31.3 0.8 copy-done.2
  32.1 2.0 %pick.1 = f32[256,512]{1,0:T(8,128)} custom-call(s32[1]{0:T(128)} %bitcast.2.which_ref, f32[1024,512]{1,0:T(8,128)} %state_ref.1, f32[256,512]{1,0:T(8,128)} %copy-done.2, f32[256,512]{1,0:T(8,128)} %slice_bitcast_fusion.refs_1_), custom_call_target="tpu_custom_call" | custom-call | bytes 1000000 | tf_op jit(solution)/shard_map/pick/pallas_call | solution.py:153
  34.1 10.2 %all-to-all-start.2 = ((f32[32,8,512]{2,1,0:T(8,128)}), f32[32,8,512]{2,1,0:T(8,128)}, u32[]{:S(2)}, u32[]{:S(2)}) async-start(f32[32,8,512]{2,1,0:T(8,128)} %bitcast.18), calls=%async_computation.2 | async-start | bytes 1048576 | tf_op jit(solution)/shard_map/all_to_all | solution.py:248
  44.4 0.0 collective-permute-done.4
  44.4 0.2 broadcast_select_fusion
  44.6 1.6 %collective-permute-start.5 = (f32[512,512]{1,0:T(8,128)S(1)}, f32[512,512]{1,0:T(8,128)}, u32[]{:S(2)}, u32[]{:S(2)}) collective-permute-start(f32[512,512]{1,0:T(8,128)S(1)} %broadcast_select_fusion), channel_id=1, source_target_pairs={{0,128},{256,384},{1,129},{257,385},{2,130},{258,386},{3,131},{259... | collective-permute-start | bytes 3145736 | tf_op jit(solution)/shard_map/ppermute | solution.py:283
  46.3 1.5 collective-permute-start
  47.7 1.4 collective-permute-start.1
  49.2 8.5 %all-to-all-done.2 = f32[32,8,512]{2,1,0:T(8,128)} async-done(((f32[32,8,512]{2,1,0:T(8,128)}), f32[32,8,512]{2,1,0:T(8,128)}, u32[]{:S(2)}, u32[]{:S(2)}) %all-to-all-start.2) | async-done | bytes 524320 | tf_op jit(solution)/shard_map/all_to_all | solution.py:248
  57.6 0.7 slice_bitcast_fusion.2
  58.4 0.7 broadcast_in_dim.23
  59.0 6.2 %all-to-all-start.3 = ((f32[8,8,512]{2,1,0:T(8,128)}), f32[8,8,512]{2,1,0:T(8,128)S(1)}, u32[]{:S(2)}, u32[]{:S(2)}) async-start(f32[8,8,512]{2,1,0:T(8,128)} %broadcast_in_dim.23), calls=%async_computation.3 | async-start | bytes 262144 | tf_op jit(solution)/shard_map/all_to_all | solution.py:253
  65.3 1.2 broadcast_select_fusion.1
  66.5 1.6 %collective-permute-start.6 = (f32[512,512]{1,0:T(8,128)}, f32[512,512]{1,0:T(8,128)}, u32[]{:S(2)}, u32[]{:S(2)}) collective-permute-start(f32[512,512]{1,0:T(8,128)} %broadcast_select_fusion.1), channel_id=1, source_target_pairs={{0,64},{128,192},{256,320},{384,448},{1,65},{129,193},{257,321},{3... | collective-permute-start | bytes 3145736 | tf_op jit(solution)/shard_map/ppermute | solution.py:283
  68.1 5.1 %all-to-all-done.3 = f32[8,8,512]{2,1,0:T(8,128)S(1)} async-done(((f32[8,8,512]{2,1,0:T(8,128)}), f32[8,8,512]{2,1,0:T(8,128)S(1)}, u32[]{:S(2)}, u32[]{:S(2)}) %all-to-all-start.3) | async-done | bytes 131104 | tf_op jit(solution)/shard_map/all_to_all | solution.py:253
  73.2 0.9 broadcast_in_dim.25
  74.1 9.5 %all-to-all-start.4 = ((f32[32,8,512]{2,1,0:T(8,128)}), f32[32,8,512]{2,1,0:T(8,128)S(1)}, u32[]{:S(2)}, u32[]{:S(2)}) async-start(f32[32,8,512]{2,1,0:T(8,128)} %broadcast_in_dim.25), calls=%async_computation.4 | async-start | bytes 1048576 | tf_op jit(solution)/shard_map/all_to_all | solution.py:253
  83.6 0.0 collective-permute-done
  83.6 0.0 collective-permute-done.1
  83.6 1.5 add_select_fusion.1
  85.2 1.5 collective-permute-start.2
  86.6 1.3 collective-permute-start.3
  87.9 0.0 collective-permute-done.2
  87.9 12.0 %collective-permute-done.3 = f32[256,512]{1,0:T(8,128)} collective-permute-done((f32[256,512]{1,0:T(8,128)S(1)}, f32[256,512]{1,0:T(8,128)}, u32[]{:S(2)}, u32[]{:S(2)}) %collective-permute-start.3) | collective-permute-done | bytes 524320 | tf_op jit(solution)/shard_map/ppermute | solution.py:270
  99.9 2.2 %add_select_fusion = f32[256,512]{1,0:T(8,128)} fusion(f32[256,512]{1,0:T(8,128)S(1)} %add_select_fusion.1, f32[256,512]{1,0:T(8,128)} %collective-permute-done.2, f32[256,512]{1,0:T(8,128)} %collective-permute-done.3, pred[]{:T(512)S(6)} %or.7), kind=kLoop, calls=%fused_computation.1 | loop fusion | flops 262144 | bytes 2097153 | tf_op jit(solution)/shard_map/jit(_where)/select_n | solution.py:271
  102.1 0.0 all-to-all-done.4
  102.1 2.6 %broadcast_in_dim.10 = f32[4,256,512]{2,1,0:T(8,128)} broadcast(f32[256,512]{1,0:T(8,128)} %add_select_fusion), dimensions={1,2} | broadcast | bytes 2621440 | tf_op jit(solution)/shard_map/broadcast_in_dim | solution.py:252
  104.7 4.7 %all-to-all-start.1 = ((f32[4,256,512]{2,1,0:T(8,128)}), f32[4,256,512]{2,1,0:T(8,128)}, u32[]{:S(2)}, u32[]{:S(2)}) async-start(f32[4,256,512]{2,1,0:T(8,128)} %broadcast_in_dim.10), calls=%async_computation.1 | async-start | bytes 4194304 | tf_op jit(solution)/shard_map/all_to_all | solution.py:253
  109.4 0.0 collective-permute-done.6
  109.4 2.4 %broadcast_select_fusion.2.tile_ref = f32[512,512]{1,0:T(8,128)} fusion(f32[512,512]{1,0:T(8,128)} %collective-permute-done.6, f32[512,512]{1,0:T(8,128)} %broadcast_select_fusion.1, pred[]{:T(512)S(6)} %eq.26), kind=kLoop, calls=%fused_computation.5 | loop fusion | flops 262144 | bytes 3145729 | tf_op jit(solution)/shard_map/jit(_where)/select_n | solution.py:284
  111.8 1.3 collective-permute-start.7
  113.1 16.6 %collective-permute-start.9 = (f32[256,512]{1,0:T(8,128)S(1)}, f32[256,512]{1,0:T(8,128)S(1)}, u32[]{:S(2)}, u32[]{:S(2)}) collective-permute-start(f32[256,512]{1,0:T(8,128)S(1)} %bitcast.16), channel_id=1, source_target_pairs={{0,32},{32,0},{1,33},{33,1},{2,34},{34,2},{3,35},{35,3},{4,36},{36... | collective-permute-start | bytes 1572872 | tf_op jit(solution)/shard_map/ppermute | solution.py:257
  129.7 0.1 pad_add_fusion.here_ref
  129.8 1.4 collective-permute-done.9.other_ref
  131.2 6.4 %factor_0.1.old_ref = f32[512,512]{1,0:T(8,128)S(1)} custom-call(s32[3]{0:T(128)S(1)} %pad_add_fusion.here_ref, f32[256,512]{1,0:T(8,128)S(1)} %bitcast.17, f32[256,512]{1,0:T(8,128)S(1)} %collective-permute-done.9.other_ref), custom_call_target="tpu_custom_call" | custom-call | flops 1000000 | bytes 100000 | tf_op jit(solution)/shard_map/factor_0/pallas_call | solution.py:128
  137.6 5.3 %factor_1.1.old_ref = f32[512,512]{1,0:T(8,128)S(1)} custom-call(f32[512,512]{1,0:T(8,128)S(1)} %factor_0.1.old_ref), custom_call_target="tpu_custom_call" | custom-call | flops 1000000 | bytes 100000 | tf_op jit(solution)/shard_map/factor_1/pallas_call | solution.py:135
  142.9 5.0 %factor_2.1.old_ref = f32[512,512]{1,0:T(8,128)S(1)} custom-call(f32[512,512]{1,0:T(8,128)S(1)} %factor_1.1.old_ref), custom_call_target="tpu_custom_call" | custom-call | flops 1000000 | bytes 100000 | tf_op jit(solution)/shard_map/factor_2/pallas_call | solution.py:135
  147.9 4.9 %factor_3.1.inverse_ref = f32[512,512]{1,0:T(8,128)S(1)} custom-call(f32[512,512]{1,0:T(8,128)S(1)} %factor_2.1.old_ref), custom_call_target="tpu_custom_call" | custom-call | flops 1000000 | bytes 100000 | tf_op jit(solution)/shard_map/factor_3/pallas_call | solution.py:135
  152.9 0.0 all-to-all-done.1
  152.9 9.0 %update.1 = f32[1024,512]{1,0:T(8,128)} custom-call(s32[3]{0:T(128)S(1)} %pad_add_fusion.here_ref, f32[1024,512]{1,0:T(8,128)S(1)} %copy-done.1, f32[1024,512]{1,0:T(8,128)} %bitcast.5.panel_ref, f32[512,512]{1,0:T(8,128)} %broadcast_select_fusion.2.tile_ref, f32[512,512]{1,0:T(8,128)} %collective-permute-done.7.sent_ref, f32[512,512]{1,0:T(8,128)S(1)} %factor_3.1.inverse_ref), custom_call_target="tpu_custom_call" | custom-call | flops 4026531840 | bytes 8388608 | tf_op jit(solution)/shard_map/update/pallas_call | solution.py:224
  (8 shorter events, 0.0 us)
Async XLA Ops:
  0.0 4.8 %copy-start = (f32[1024,512]{1,0:T(8,128)S(1)}, f32[1024,512]{1,0:T(8,128)}, u32[]{:S(2)}) copy-start(f32[1024,512]{1,0:T(8,128)} %state_ref.1) | copy-start | bytes 6291460
  0.0 29.5 %all-to-all-start = ((f32[4,256,512]{2,1,0:T(8,128)}), f32[4,256,512]{2,1,0:T(8,128)}, u32[]{:S(2)}, u32[]{:S(2)}) async-start(f32[4,256,512]{2,1,0:T(8,128)} %bitcast.15), calls=%async_computation | async-start | bytes 4194304 | tf_op jit(solution)/shard_map/all_to_all | solution.py:248
  4.9 39.5 %collective-permute-start.4 = (f32[512,512]{1,0:T(8,128)S(1)}, f32[512,512]{1,0:T(8,128)}, u32[]{:S(2)}, u32[]{:S(2)}) collective-permute-start(f32[512,512]{1,0:T(8,128)S(1)} %slice.17), channel_id=1, source_target_pairs={{0,256},{1,257},{2,258},{3,259},{4,260},{5,261},{6,262},{7,263},{8... | collective-permute-start | bytes 3145736 | tf_op jit(solution)/shard_map/ppermute | solution.py:283
  7.4 24.0 %collective-permute-start.8 = (f32[256,512]{1,0:T(8,128)}, f32[256,512]{1,0:T(8,128)S(1)}, u32[]{:S(2)}, u32[]{:S(2)}) collective-permute-start(f32[256,512]{1,0:T(8,128)} %slice.18), channel_id=1, source_target_pairs={{0,32},{32,0},{1,33},{33,1},{2,34},{34,2},{3,35},{35,3},{4,36},{36... | collective-permute-start | bytes 1572872 | tf_op jit(solution)/shard_map/ppermute | solution.py:257
  31.3 0.8 copy-start.2
  32.1 12.2 %copy-start.1 = (f32[1024,512]{1,0:T(8,128)S(1)}, f32[1024,512]{1,0:T(8,128)}, u32[]{:S(2)}) copy-start(f32[1024,512]{1,0:T(8,128)} %state_ref.1) | copy-start | bytes 6291460
  34.1 23.5 %all-to-all-start.2 = ((f32[32,8,512]{2,1,0:T(8,128)}), f32[32,8,512]{2,1,0:T(8,128)}, u32[]{:S(2)}, u32[]{:S(2)}) async-start(f32[32,8,512]{2,1,0:T(8,128)} %bitcast.18), calls=%async_computation.2 | async-start | bytes 1048576 | tf_op jit(solution)/shard_map/all_to_all | solution.py:248
  44.6 20.7 %collective-permute-start.5 = (f32[512,512]{1,0:T(8,128)S(1)}, f32[512,512]{1,0:T(8,128)}, u32[]{:S(2)}, u32[]{:S(2)}) collective-permute-start(f32[512,512]{1,0:T(8,128)S(1)} %broadcast_select_fusion), channel_id=1, source_target_pairs={{0,128},{256,384},{1,129},{257,385},{2,130},{258,386},{3,131},{259... | collective-permute-start | bytes 3145736 | tf_op jit(solution)/shard_map/ppermute | solution.py:283
  46.3 37.4 %collective-permute-start = (f32[256,512]{1,0:T(8,128)}, f32[256,512]{1,0:T(8,128)}, u32[]{:S(2)}, u32[]{:S(2)}) collective-permute-start(f32[256,512]{1,0:T(8,128)} %slice_bitcast_fusion.refs_1_), channel_id=1, source_target_pairs={{0,12},{1,13},{2,14},{3,15},{32,44},{33,45},{34,46},{35,47},{64,76... | collective-permute-start | bytes 1572872 | tf_op jit(solution)/shard_map/ppermute | solution.py:267
  47.7 35.9 %collective-permute-start.1 = (f32[256,512]{1,0:T(8,128)}, f32[256,512]{1,0:T(8,128)}, u32[]{:S(2)}, u32[]{:S(2)}) collective-permute-start(f32[256,512]{1,0:T(8,128)} %slice_bitcast_fusion.refs_1_), channel_id=1, source_target_pairs={{0,20},{1,21},{2,22},{3,23},{32,52},{33,53},{34,54},{35,55},{64,84... | collective-permute-start | bytes 1572872 | tf_op jit(solution)/shard_map/ppermute | solution.py:267
  59.0 14.2 %all-to-all-start.3 = ((f32[8,8,512]{2,1,0:T(8,128)}), f32[8,8,512]{2,1,0:T(8,128)S(1)}, u32[]{:S(2)}, u32[]{:S(2)}) async-start(f32[8,8,512]{2,1,0:T(8,128)} %broadcast_in_dim.23), calls=%async_computation.3 | async-start | bytes 262144 | tf_op jit(solution)/shard_map/all_to_all | solution.py:253
  66.5 42.9 %collective-permute-start.6 = (f32[512,512]{1,0:T(8,128)}, f32[512,512]{1,0:T(8,128)}, u32[]{:S(2)}, u32[]{:S(2)}) collective-permute-start(f32[512,512]{1,0:T(8,128)} %broadcast_select_fusion.1), channel_id=1, source_target_pairs={{0,64},{128,192},{256,320},{384,448},{1,65},{129,193},{257,321},{3... | collective-permute-start | bytes 3145736 | tf_op jit(solution)/shard_map/ppermute | solution.py:283
  74.1 28.0 %all-to-all-start.4 = ((f32[32,8,512]{2,1,0:T(8,128)}), f32[32,8,512]{2,1,0:T(8,128)S(1)}, u32[]{:S(2)}, u32[]{:S(2)}) async-start(f32[32,8,512]{2,1,0:T(8,128)} %broadcast_in_dim.25), calls=%async_computation.4 | async-start | bytes 1048576 | tf_op jit(solution)/shard_map/all_to_all | solution.py:253
  85.2 2.8 %collective-permute-start.2 = (f32[256,512]{1,0:T(8,128)S(1)}, f32[256,512]{1,0:T(8,128)}, u32[]{:S(2)}, u32[]{:S(2)}) collective-permute-start(f32[256,512]{1,0:T(8,128)S(1)} %add_select_fusion.1), channel_id=1, source_target_pairs={{0,4},{12,16},{20,24},{1,5},{13,17},{21,25},{2,6},{14,18},{22,26},... | collective-permute-start | bytes 1572872 | tf_op jit(solution)/shard_map/ppermute | solution.py:269
  86.6 13.3 %collective-permute-start.3 = (f32[256,512]{1,0:T(8,128)S(1)}, f32[256,512]{1,0:T(8,128)}, u32[]{:S(2)}, u32[]{:S(2)}) collective-permute-start(f32[256,512]{1,0:T(8,128)S(1)} %add_select_fusion.1), channel_id=1, source_target_pairs={{0,28},{12,8},{1,29},{13,9},{2,30},{14,10},{3,31},{15,11},{32,60},... | collective-permute-start | bytes 1572872 | tf_op jit(solution)/shard_map/ppermute | solution.py:270
  104.7 48.2 %all-to-all-start.1 = ((f32[4,256,512]{2,1,0:T(8,128)}), f32[4,256,512]{2,1,0:T(8,128)}, u32[]{:S(2)}, u32[]{:S(2)}) async-start(f32[4,256,512]{2,1,0:T(8,128)} %broadcast_in_dim.10), calls=%async_computation.1 | async-start | bytes 4194304 | tf_op jit(solution)/shard_map/all_to_all | solution.py:253
  111.8 41.1 %collective-permute-start.7 = (f32[512,512]{1,0:T(8,128)}, f32[512,512]{1,0:T(8,128)}, u32[]{:S(2)}, u32[]{:S(2)}) collective-permute-start(f32[512,512]{1,0:T(8,128)} %broadcast_select_fusion.2.tile_ref), channel_id=1, source_target_pairs={{0,32},{1,33},{2,34},{3,35},{4,36},{5,37},{6,38},{7,39},{8,40},{9,... | collective-permute-start | bytes 3145736 | tf_op jit(solution)/shard_map/ppermute | solution.py:285
  113.1 18.1 %collective-permute-start.9 = (f32[256,512]{1,0:T(8,128)S(1)}, f32[256,512]{1,0:T(8,128)S(1)}, u32[]{:S(2)}, u32[]{:S(2)}) collective-permute-start(f32[256,512]{1,0:T(8,128)S(1)} %bitcast.16), channel_id=1, source_target_pairs={{0,32},{32,0},{1,33},{33,1},{2,34},{34,2},{3,35},{35,3},{4,36},{36... | collective-permute-start | bytes 1572872 | tf_op jit(solution)/shard_map/ppermute | solution.py:257

commit v4 on v2

--- a/solution.py
+++ b/solution.py
@@ -96,30 +96,51 @@
         v_ref[there, :] -= _dot(v_ref[here, there].T, v_ref[here, :])
 
 
-def _factor_kernel(k, old_ref, v_ref):
+def _factor_kernel(k, old_ref, *refs):
+    v_ref = refs[-1]
     v_ref[...] = old_ref[...]
     _eliminate(k, v_ref)
 
 
-def factor_inverse(covariance):
+def _last_kernel(old_ref, upper_ref, lower_ref, v_ref):
+    _factor_kernel(NB // BK - 1, old_ref, v_ref)
+    upper_ref[...] = v_ref[: NB // 2, :]
+    lower_ref[...] = v_ref[NB // 2 :, :]
+
+
+def factor_inverse(covariance, after):
     state = covariance
-    for k in range(NB // BK):
+    whole = pl.BlockSpec((NB, NB), lambda i: (0, 0))
+    half = pl.BlockSpec((NB // 2, NB), lambda i: (0, 0))
+    rest = dict(
+        grid=(1,),
+        compiler_params=pltpu.CompilerParams(vmem_limit_bytes=24 * 2**20),
+        cost_estimate=pl.CostEstimate(flops=10**6, bytes_accessed=10**5, transcendentals=NB),
+    )
+    for k in range(NB // BK - 1):
+        extra = (after,) if k == 2 else ()
         state = pl.pallas_call(
             functools.partial(_factor_kernel, k),
-            grid=(1,),
             out_shape=jax.ShapeDtypeStruct((NB, NB), jnp.float32),
-            in_specs=[pl.BlockSpec((NB, NB), lambda i: (0, 0))],
-            out_specs=pl.BlockSpec((NB, NB), lambda i: (0, 0)),
-            compiler_params=pltpu.CompilerParams(vmem_limit_bytes=24 * 2**20),
-            cost_estimate=pl.CostEstimate(flops=10**6, bytes_accessed=10**5, transcendentals=NB),
+            in_specs=[whole] + [pl.BlockSpec(memory_space=pl.ANY)] * len(extra),
+            out_specs=whole,
             name=f"factor_{k}",
-        )(state)
-    return state
-
-
-def _pick_kernel(which_ref, first_ref, *refs):
-    *others, o_ref, sem = refs
-    for i, ref in enumerate((first_ref.at[: o_ref.shape[0]], *others)):
+            **rest,
+        )(state, *extra)
+    return pl.pallas_call(
+        _last_kernel,
+        out_shape=[jax.ShapeDtypeStruct((NB // 2, NB), jnp.float32)] * 2,
+        in_specs=[whole],
+        out_specs=[half, half],
+        scratch_shapes=[pltpu.VMEM((NB, NB), jnp.float32)],
+        name="factor_3",
+        **rest,
+    )(state)
+
+
+def _pick_kernel(count, which_ref, *refs):
+    *_, o_ref, sem = refs
+    for i, ref in enumerate(refs[:count]):
 
         @pl.when(which_ref[0] == i)
         def _():
@@ -128,17 +149,18 @@
             copy.wait()
 
 
-def pick(which, first, *others):
+def pick(which, arrays, after):
+    operands = (*arrays, *after)
     return pl.pallas_call(
-        _pick_kernel,
-        out_shape=jax.ShapeDtypeStruct(others[0].shape, jnp.float32),
+        functools.partial(_pick_kernel, len(arrays)),
+        out_shape=jax.ShapeDtypeStruct(arrays[0].shape, jnp.float32),
         in_specs=[pl.BlockSpec(memory_space=pltpu.SMEM)]
-        + [pl.BlockSpec(memory_space=pl.ANY)] * (1 + len(others)),
+        + [pl.BlockSpec(memory_space=pl.ANY)] * len(operands),
         out_specs=pl.BlockSpec(memory_space=pltpu.VMEM),
         scratch_shapes=[pltpu.SemaphoreType.DMA],
         cost_estimate=pl.CostEstimate(flops=0, bytes_accessed=10**6, transcendentals=0),
         name="pick",
-    )(which.reshape(1), first, *others)
+    )(which.reshape(1), *operands)
 
 
 def _split(value):
@@ -261,19 +283,21 @@
 def body(covariance):
     ny, nz, nx = (lax.axis_size(axis) for axis in ("y", "z", "x"))
     core, x, y, z = (lax.axis_index(axis) for axis in ("core", "x", "y", "z"))
-    half = NB // 2
     here = jnp.stack([y * 2 + core, z * nx + x, core, x]).astype(jnp.int32)
 
-    inverse = factor_inverse(covariance)
-    mine = pick(core, inverse, swap_cores(inverse[half:]))
-    part = send_parts(mine, ("z", "x"), nz * nx)
-    part = gather(part, "y", ny)[: part.shape[0]]
-    mine = gather(part, ("z", "x"), nz * nx)
-    inverse = mine, swap_cores(mine)
+    mirror = covariance[:NB]
+    rounds = []
+    for step in (4, 2, 1):
+        pairs = [(2 * i, 2 * (i + step)) for i in range(0, ny, 2 * step)]
+        sent = lax.ppermute(mirror, ("y", "core"), pairs)
+        mirror = jnp.where(y % (2 * step) == step, sent, mirror)
+        rounds.append(mirror)
+    mirror = mirror, lax.ppermute(mirror, "core", [(0, 1)])
 
     quarter = send_parts(covariance, "x", nx)
-    spread = lax.ppermute(quarter, "z", [(0, 3)]) + lax.ppermute(quarter, "z", [(0, 5)])
-    spread = jnp.where(z == 0, quarter, spread)
+    third = lax.ppermute(quarter, "z", [(0, 3)])
+    fifth = lax.ppermute(quarter, "z", [(0, 5)])
+    spread = jnp.where(z == 0, quarter, third + fifth)
     own = lax.ppermute(spread, "z", [(0, 1), (3, 4), (5, 6)])
     own = own + lax.ppermute(spread, "z", [(0, 7), (3, 2)])
     own = jnp.where((z == 0) | (z == 3) | (z == 5), spread, own)
@@ -285,12 +309,12 @@
     top = lax.ppermute(back[:rest], "x", ring)
     low = lax.ppermute(ahead[rest:], "x", back_ring)
 
-    mirror = covariance[:NB]
-    for step in (4, 2, 1):
-        pairs = [(2 * i, 2 * (i + step)) for i in range(0, ny, 2 * step)]
-        sent = lax.ppermute(mirror, ("y", "core"), pairs)
-        mirror = jnp.where(y % (2 * step) == step, sent, mirror)
-    mirror = mirror, lax.ppermute(mirror, "core", [(0, 1)])
+    upper, lower = factor_inverse(covariance, rounds[0])
+    mine = pick(core, (upper, swap_cores(lower)), (third, fifth))
+    part = send_parts(mine, ("z", "x"), nz * nx)
+    part = gather(part, "y", ny)[: part.shape[0]]
+    mine = gather(part, ("z", "x"), nz * nx)
+    inverse = mine, swap_cores(mine)
     return update(here, covariance, (own, back, top, low, ahead), mirror, inverse)
 
 

time: 150 us -> 170 us (1.13)
  the two profiles are of different devices: /device:TPU:64 before, /device:TPU:72 now
where the time goes in v4:
time: 170 us; the launch traced here: 169 us
  starting transfers between devices  85.7 us (50%)
  waiting for transfers between devices  34.7 us (20%)
  Pallas kernels  32.4 us (19%)
  local copies, waits for them, and re-layouts  8.32 us (5%)
  other arithmetic  7.38 us (4%)
    all_to_all x2, starting transfers between devices, send_parts(): lax.all_to_all(value.reshape(parts, size, value.shape[1]), axis, 0, 0)[0]  33.1 us
    all_to_all x2, starting transfers between devices, gather(): return lax.all_to_all(copies, axis, 0, 0).reshape(-1, value.shape[1])  22.2 us
    pallas_call x3, Pallas kernels, factor_inverse(): pl.pallas_call(functools.partial(_factor_kernel, k), out_shape=jax.ShapeD...  15.8 us
    all_to_all x2, waiting for transfers between devices, send_parts(): lax.all_to_all(value.reshape(parts, size, value.shape[1]), axis, 0, 0)[0]  15 us
    pallas_call x1, Pallas kernels, update(): pl.pallas_call(_update_kernel, grid=(state.shape[0] // CHUNK,), out_shape...  9.01 us
    ppermute x1, waiting for transfers between devices, body(): top = lax.ppermute(back[:rest], 'x', ring)  7.28 us
    ppermute x1, waiting for transfers between devices, body(): own = lax.ppermute(spread, 'z', [(0, 1), (3, 4), (5, 6)])  6.17 us
    pallas_call x1, Pallas kernels, factor_inverse(): pl.pallas_call(_last_kernel, out_shape=[jax.ShapeDtypeStruct((NB // 2, NB...  5.7 us
  transfers between devices with their start and end apart: 18, of which 7 were waited for; matrix products, arithmetic and copies ran while one was open for 9% of the time, Pallas kernels for 14%

profile of v4, /device:TPU:72, one launch (start us, length us, event | category | flops | bytes accessed | tf_op | source)
XLA Modules:
  0.0 168.9 jit_solution(6805122593887052831)
XLA Ops:
  0.0 4.6 %all-to-all-start = ((f32[4,256,512]{2,1,0:T(8,128)}), f32[4,256,512]{2,1,0:T(8,128)}, u32[]{:S(2)}, u32[]{:S(2)}) async-start(f32[4,256,512]{2,1,0:T(8,128)} %bitcast.15), calls=%async_computation | async-start | bytes 4194304 | tf_op jit(solution)/shard_map/all_to_all | solution.py:271
  4.6 0.1 slice.22
  4.7 1.7 collective-permute-start.8
  6.4 5.5 %factor_0.1.old_ref = f32[512,512]{1,0:T(8,128)S(1)} custom-call(f32[1024,512]{1,0:T(8,128)S(1)} %copy-done), custom_call_target="tpu_custom_call" | custom-call | flops 1000000 | bytes 100000 | tf_op jit(solution)/shard_map/factor_0/pallas_call | solution.py:122
  11.9 5.3 %factor_1.1.old_ref = f32[512,512]{1,0:T(8,128)S(1)} custom-call(f32[512,512]{1,0:T(8,128)S(1)} %factor_0.1.old_ref), custom_call_target="tpu_custom_call" | custom-call | flops 1000000 | bytes 100000 | tf_op jit(solution)/shard_map/factor_1/pallas_call | solution.py:122
  17.2 0.0 collective-permute-done.8
  17.2 0.2 broadcast_select_fusion.refs_0_
  17.4 5.0 %factor_2.1.old_ref = f32[512,512]{1,0:T(8,128)S(1)} custom-call(f32[512,512]{1,0:T(8,128)S(1)} %factor_1.1.old_ref, f32[512,512]{1,0:T(8,128)S(1)} %broadcast_select_fusion.refs_0_), custom_call_target="tpu_custom_call" | custom-call | flops 1000000 | bytes 100000 | tf_op jit(solution)/shard_map/factor_2/pallas_call | solution.py:122
  22.4 5.7 %factor_3.1 = (f32[256,512]{1,0:T(8,128)S(1)}, f32[256,512]{1,0:T(8,128)}) custom-call(f32[512,512]{1,0:T(8,128)S(1)} %factor_2.1.old_ref), custom_call_target="tpu_custom_call" | custom-call | flops 1000000 | bytes 100000 | tf_op jit(solution)/shard_map/factor_3/pallas_call | solution.py:130
  28.1 0.8 copy-done.1
  28.9 1.9 %collective-permute-start.12 = (f32[256,512]{1,0:T(8,128)}, f32[256,512]{1,0:T(8,128)}, u32[]{:S(2)}, u32[]{:S(2)}) collective-permute-start(f32[256,512]{1,0:T(8,128)} %get-tuple-element.8), channel_id=1, source_target_pairs={{0,32},{32,0},{1,33},{33,1},{2,34},{34,2},{3,35},{35,3},{4,36},{36... | collective-permute-start | bytes 1572872 | tf_op jit(solution)/shard_map/ppermute | solution.py:280
  30.8 0.4 all-to-all-done
  31.3 1.9 %slice_bitcast_fusion = f32[256,512]{1,0:T(8,128)} fusion(f32[4,256,512]{2,1,0:T(8,128)} %all-to-all-done), kind=kLoop, calls=%fused_computation | loop fusion | bytes 1048576 | tf_op jit(solution)/shard_map/squeeze | solution.py:271
  33.1 1.4 collective-permute-start.1
  34.6 1.5 collective-permute-start
  36.0 1.6 collective-permute-start.9
  37.7 0.0 collective-permute-done.refs_2_
  37.7 1.9 %pick.1 = f32[256,512]{1,0:T(8,128)} custom-call(s32[1]{0:T(128)} %bitcast.2.which_ref, f32[256,512]{1,0:T(8,128)} %copy-done.1, f32[256,512]{1,0:T(8,128)} %collective-permute-done.12.refs_1_, f32[256,512]{1,0:T(8,128)} %collective-permute-done.refs_2_, f32[256,512]{1,0:T(8,128)} %collective-permute-done.1.refs_3_), custom_call_target="tpu_custom_call" | custom-call | bytes 1000000 | tf_op jit(solution)/shard_map/pick/pallas_call | solution.py:154
  39.6 28.5 %all-to-all-start.1 = ((f32[32,8,512]{2,1,0:T(8,128)}), f32[32,8,512]{2,1,0:T(8,128)}, u32[]{:S(2)}, u32[]{:S(2)}) async-start(f32[32,8,512]{2,1,0:T(8,128)} %bitcast.16), calls=%async_computation.1 | async-start | bytes 1048576 | tf_op jit(solution)/shard_map/all_to_all | solution.py:271
  68.1 1.2 broadcast_select_fusion.1
  69.3 1.3 collective-permute-start.10
  70.6 14.6 %all-to-all-done.1 = f32[32,8,512]{2,1,0:T(8,128)} async-done(((f32[32,8,512]{2,1,0:T(8,128)}), f32[32,8,512]{2,1,0:T(8,128)}, u32[]{:S(2)}, u32[]{:S(2)}) %all-to-all-start.1) | async-done | bytes 524320 | tf_op jit(solution)/shard_map/all_to_all | solution.py:271
  85.2 0.7 slice_bitcast_fusion.2
  85.9 0.7 broadcast_in_dim.16
  86.6 16.9 %all-to-all-start.2 = ((f32[8,8,512]{2,1,0:T(8,128)}), f32[8,8,512]{2,1,0:T(8,128)S(1)}, u32[]{:S(2)}, u32[]{:S(2)}) async-start(f32[8,8,512]{2,1,0:T(8,128)} %broadcast_in_dim.16), calls=%async_computation.2 | async-start | bytes 262144 | tf_op jit(solution)/shard_map/all_to_all | solution.py:276
  103.5 2.3 %add_select_fusion.1 = f32[256,512]{1,0:T(8,128)} fusion(f32[256,512]{1,0:T(8,128)} %collective-permute-done.refs_2_, f32[256,512]{1,0:T(8,128)} %collective-permute-done.1.refs_3_, pred[]{:T(512)S(6)} %eq.23, f32[4,256,512]{2,1,0:T(8,128)} %all-to-all-done), kind=kLoop, calls=%fused_computation.2 | loop fusion | flops 262144 | bytes 2097153 | tf_op jit(solution)/shard_map/jit(_where)/select_n | solution.py:300
  105.8 1.4 collective-permute-start.3
  107.3 1.3 collective-permute-start.2
  108.6 2.6 %all-to-all-done.2 = f32[8,8,512]{2,1,0:T(8,128)S(1)} async-done(((f32[8,8,512]{2,1,0:T(8,128)}), f32[8,8,512]{2,1,0:T(8,128)S(1)}, u32[]{:S(2)}, u32[]{:S(2)}) %all-to-all-start.2) | async-done | bytes 131104 | tf_op jit(solution)/shard_map/all_to_all | solution.py:276
  111.2 0.9 broadcast_in_dim.18
  112.0 5.3 %all-to-all-start.3 = ((f32[32,8,512]{2,1,0:T(8,128)}), f32[32,8,512]{2,1,0:T(8,128)}, u32[]{:S(2)}, u32[]{:S(2)}) async-start(f32[32,8,512]{2,1,0:T(8,128)} %broadcast_in_dim.18), calls=%async_computation.3 | async-start | bytes 1048576 | tf_op jit(solution)/shard_map/all_to_all | solution.py:276
  117.3 0.0 collective-permute-done.10
  117.3 1.4 broadcast_select_fusion.2.tile_ref
  118.8 2.3 %collective-permute-start.11 = (f32[512,512]{1,0:T(8,128)S(1)}, f32[512,512]{1,0:T(8,128)}, u32[]{:S(2)}, u32[]{:S(2)}) collective-permute-start(f32[512,512]{1,0:T(8,128)S(1)} %broadcast_select_fusion.2.tile_ref), channel_id=1, source_target_pairs={{0,32},{1,33},{2,34},{3,35},{4,36},{5,37},{6,38},{7,39},{8,40},{9,... | collective-permute-start | bytes 3145736 | tf_op jit(solution)/shard_map/ppermute | solution.py:295
  121.1 6.2 %collective-permute-done.2 = f32[256,512]{1,0:T(8,128)} collective-permute-done((f32[256,512]{1,0:T(8,128)}, f32[256,512]{1,0:T(8,128)}, u32[]{:S(2)}, u32[]{:S(2)}) %collective-permute-start.2) | collective-permute-done | bytes 524320 | tf_op jit(solution)/shard_map/ppermute | solution.py:301
  127.2 2.1 %add_select_fusion.own_ref = f32[256,512]{1,0:T(8,128)} fusion(f32[256,512]{1,0:T(8,128)} %add_select_fusion.1, f32[256,512]{1,0:T(8,128)} %collective-permute-done.2, f32[256,512]{1,0:T(8,128)} %collective-permute-done.3, pred[]{:T(512)S(6)} %or.7), kind=kLoop, calls=%fused_computation.1 | loop fusion | flops 262144 | bytes 2097153 | tf_op jit(solution)/shard_map/jit(_where)/select_n | solution.py:303
  129.4 4.6 %collective-permute-start.6 = (f32[256,512]{1,0:T(8,128)}, f32[256,512]{1,0:T(8,128)}, u32[]{:S(2)}, u32[]{:S(2)}) collective-permute-start(f32[256,512]{1,0:T(8,128)} %add_select_fusion.own_ref), channel_id=1, source_target_pairs={{1,0},{2,1},{3,2},{0,3},{5,4},{6,5},{7,6},{4,7},{9,8},{10,9},{11,1... | collective-permute-start | bytes 1572872 | tf_op jit(solution)/shard_map/ppermute | solution.py:307
  134.0 1.9 %collective-permute-start.4 = (f32[256,512]{1,0:T(8,128)}, f32[256,512]{1,0:T(8,128)}, u32[]{:S(2)}, u32[]{:S(2)}) collective-permute-start(f32[256,512]{1,0:T(8,128)} %add_select_fusion.own_ref), channel_id=1, source_target_pairs={{0,1},{1,2},{2,3},{3,0},{4,5},{5,6},{6,7},{7,4},{8,9},{9,10},{10,1... | collective-permute-start | bytes 1572872 | tf_op jit(solution)/shard_map/ppermute | solution.py:306
  136.0 1.9 %collective-permute-start.13 = (f32[256,512]{1,0:T(8,128)}, f32[256,512]{1,0:T(8,128)}, u32[]{:S(2)}, u32[]{:S(2)}) collective-permute-start(f32[256,512]{1,0:T(8,128)} %bitcast.9.mine_ref), channel_id=1, source_target_pairs={{0,32},{32,0},{1,33},{33,1},{2,34},{34,2},{3,35},{35,3},{4,36},{36... | collective-permute-start | bytes 1572872 | tf_op jit(solution)/shard_map/ppermute | solution.py:280
  137.9 3.1 %collective-permute-done.6.ahead_ref = f32[256,512]{1,0:T(8,128)} collective-permute-done((f32[256,512]{1,0:T(8,128)}, f32[256,512]{1,0:T(8,128)}, u32[]{:S(2)}, u32[]{:S(2)}) %collective-permute-start.6) | collective-permute-done | bytes 524320 | tf_op jit(solution)/shard_map/ppermute | solution.py:307
  141.0 1.7 slice.27
  142.7 5.6 %collective-permute-start.7 = (f32[128,512]{1,0:T(8,128)}, f32[128,512]{1,0:T(8,128)S(1)}, u32[]{:S(2)}, u32[]{:S(2)}) collective-permute-start(f32[128,512]{1,0:T(8,128)} %slice.27), channel_id=1, source_target_pairs={{1,0},{2,1},{3,2},{0,3},{5,4},{6,5},{7,6},{4,7},{9,8},{10,9},{11,1... | collective-permute-start | bytes 786440 | tf_op jit(solution)/shard_map/ppermute | solution.py:310
  148.3 1.7 slice.26
  150.0 1.9 %collective-permute-start.5 = (f32[128,512]{1,0:T(8,128)}, f32[128,512]{1,0:T(8,128)}, u32[]{:S(2)}, u32[]{:S(2)}) collective-permute-start(f32[128,512]{1,0:T(8,128)} %slice.26), channel_id=1, source_target_pairs={{0,1},{1,2},{2,3},{3,0},{4,5},{5,6},{6,7},{7,4},{8,9},{9,10},{10,1... | collective-permute-start | bytes 786440 | tf_op jit(solution)/shard_map/ppermute | solution.py:309
  151.9 0.1 pad_add_fusion.here_ref
  152.0 0.5 collective-permute-done.7.low_ref
  152.5 7.3 %collective-permute-done.5.top_ref = f32[128,512]{1,0:T(8,128)} collective-permute-done((f32[128,512]{1,0:T(8,128)}, f32[128,512]{1,0:T(8,128)}, u32[]{:S(2)}, u32[]{:S(2)}) %collective-permute-start.5) | collective-permute-done | bytes 262176 | tf_op jit(solution)/shard_map/ppermute | solution.py:309
  159.7 9.0 %update.1 = f32[1024,512]{1,0:T(8,128)} custom-call(s32[4]{0:T(128)S(1)} %pad_add_fusion.here_ref, f32[1024,512]{1,0:T(8,128)S(1)} %copy-done, f32[256,512]{1,0:T(8,128)} %add_select_fusion.own_ref, f32[256,512]{1,0:T(8,128)} %collective-permute-done.4.back_ref, f32[128,512]{1,0:T(8,128)} %collective-permute-done.5.top_ref, ...), custom_call_target="tpu_custom_call" | custom-call | flops 4026531840 | bytes 8388608 | tf_op jit(solution)/shard_map/update/pallas_call | solution.py:245
  (12 shorter events, 0.0 us)
Async XLA Ops:
  0.0 4.6 %copy-start = (f32[1024,512]{1,0:T(8,128)S(1)}, f32[1024,512]{1,0:T(8,128)}, u32[]{:S(2)}) copy-start(f32[1024,512]{1,0:T(8,128)} %state_ref.1) | copy-start | bytes 6291460
  0.0 31.3 %all-to-all-start = ((f32[4,256,512]{2,1,0:T(8,128)}), f32[4,256,512]{2,1,0:T(8,128)}, u32[]{:S(2)}, u32[]{:S(2)}) async-start(f32[4,256,512]{2,1,0:T(8,128)} %bitcast.15), calls=%async_computation | async-start | bytes 4194304 | tf_op jit(solution)/shard_map/all_to_all | solution.py:271
  4.7 12.5 %collective-permute-start.8 = (f32[512,512]{1,0:T(8,128)S(1)}, f32[512,512]{1,0:T(8,128)}, u32[]{:S(2)}, u32[]{:S(2)}) collective-permute-start(f32[512,512]{1,0:T(8,128)S(1)} %slice.22), channel_id=1, source_target_pairs={{0,256},{1,257},{2,258},{3,259},{4,260},{5,261},{6,262},{7,263},{8... | collective-permute-start | bytes 3145736 | tf_op jit(solution)/shard_map/ppermute | solution.py:292
  28.1 0.8 copy-start.1
  28.9 8.8 %collective-permute-start.12 = (f32[256,512]{1,0:T(8,128)}, f32[256,512]{1,0:T(8,128)}, u32[]{:S(2)}, u32[]{:S(2)}) collective-permute-start(f32[256,512]{1,0:T(8,128)} %get-tuple-element.8), channel_id=1, source_target_pairs={{0,32},{32,0},{1,33},{33,1},{2,34},{34,2},{3,35},{35,3},{4,36},{36... | collective-permute-start | bytes 1572872 | tf_op jit(solution)/shard_map/ppermute | solution.py:280
  33.1 4.6 %collective-permute-start.1 = (f32[256,512]{1,0:T(8,128)}, f32[256,512]{1,0:T(8,128)}, u32[]{:S(2)}, u32[]{:S(2)}) collective-permute-start(f32[256,512]{1,0:T(8,128)} %slice_bitcast_fusion), channel_id=1, source_target_pairs={{0,20},{1,21},{2,22},{3,23},{32,52},{33,53},{34,54},{35,55},{64,84... | collective-permute-start | bytes 1572872 | tf_op jit(solution)/shard_map/ppermute | solution.py:299
  34.6 3.1 %collective-permute-start = (f32[256,512]{1,0:T(8,128)}, f32[256,512]{1,0:T(8,128)}, u32[]{:S(2)}, u32[]{:S(2)}) collective-permute-start(f32[256,512]{1,0:T(8,128)} %slice_bitcast_fusion), channel_id=1, source_target_pairs={{0,12},{1,13},{2,14},{3,15},{32,44},{33,45},{34,46},{35,47},{64,76... | collective-permute-start | bytes 1572872 | tf_op jit(solution)/shard_map/ppermute | solution.py:298
  36.0 32.0 %collective-permute-start.9 = (f32[512,512]{1,0:T(8,128)S(1)}, f32[512,512]{1,0:T(8,128)}, u32[]{:S(2)}, u32[]{:S(2)}) collective-permute-start(f32[512,512]{1,0:T(8,128)S(1)} %broadcast_select_fusion.refs_0_), channel_id=1, source_target_pairs={{0,128},{256,384},{1,129},{257,385},{2,130},{258,386},{3,131},{259... | collective-permute-start | bytes 3145736 | tf_op jit(solution)/shard_map/ppermute | solution.py:292
  39.6 45.6 %all-to-all-start.1 = ((f32[32,8,512]{2,1,0:T(8,128)}), f32[32,8,512]{2,1,0:T(8,128)}, u32[]{:S(2)}, u32[]{:S(2)}) async-start(f32[32,8,512]{2,1,0:T(8,128)} %bitcast.16), calls=%async_computation.1 | async-start | bytes 1048576 | tf_op jit(solution)/shard_map/all_to_all | solution.py:271
  69.3 48.0 %collective-permute-start.10 = (f32[512,512]{1,0:T(8,128)}, f32[512,512]{1,0:T(8,128)}, u32[]{:S(2)}, u32[]{:S(2)}) collective-permute-start(f32[512,512]{1,0:T(8,128)} %broadcast_select_fusion.1), channel_id=1, source_target_pairs={{0,64},{128,192},{256,320},{384,448},{1,65},{129,193},{257,321},{3... | collective-permute-start | bytes 3145736 | tf_op jit(solution)/shard_map/ppermute | solution.py:292
  86.6 24.6 %all-to-all-start.2 = ((f32[8,8,512]{2,1,0:T(8,128)}), f32[8,8,512]{2,1,0:T(8,128)S(1)}, u32[]{:S(2)}, u32[]{:S(2)}) async-start(f32[8,8,512]{2,1,0:T(8,128)} %broadcast_in_dim.16), calls=%async_computation.2 | async-start | bytes 262144 | tf_op jit(solution)/shard_map/all_to_all | solution.py:276
  105.8 15.2 %collective-permute-start.3 = (f32[256,512]{1,0:T(8,128)}, f32[256,512]{1,0:T(8,128)}, u32[]{:S(2)}, u32[]{:S(2)}) collective-permute-start(f32[256,512]{1,0:T(8,128)} %add_select_fusion.1), channel_id=1, source_target_pairs={{0,28},{12,8},{1,29},{13,9},{2,30},{14,10},{3,31},{15,11},{32,60},... | collective-permute-start | bytes 1572872 | tf_op jit(solution)/shard_map/ppermute | solution.py:302
  107.3 20.0 %collective-permute-start.2 = (f32[256,512]{1,0:T(8,128)}, f32[256,512]{1,0:T(8,128)}, u32[]{:S(2)}, u32[]{:S(2)}) collective-permute-start(f32[256,512]{1,0:T(8,128)} %add_select_fusion.1), channel_id=1, source_target_pairs={{0,4},{12,16},{20,24},{1,5},{13,17},{21,25},{2,6},{14,18},{22,26},... | collective-permute-start | bytes 1572872 | tf_op jit(solution)/shard_map/ppermute | solution.py:301
  112.0 23.9 %all-to-all-start.3 = ((f32[32,8,512]{2,1,0:T(8,128)}), f32[32,8,512]{2,1,0:T(8,128)}, u32[]{:S(2)}, u32[]{:S(2)}) async-start(f32[32,8,512]{2,1,0:T(8,128)} %broadcast_in_dim.18), calls=%async_computation.3 | async-start | bytes 1048576 | tf_op jit(solution)/shard_map/all_to_all | solution.py:276
  118.8 41.0 %collective-permute-start.11 = (f32[512,512]{1,0:T(8,128)S(1)}, f32[512,512]{1,0:T(8,128)}, u32[]{:S(2)}, u32[]{:S(2)}) collective-permute-start(f32[512,512]{1,0:T(8,128)S(1)} %broadcast_select_fusion.2.tile_ref), channel_id=1, source_target_pairs={{0,32},{1,33},{2,34},{3,35},{4,36},{5,37},{6,38},{7,39},{8,40},{9,... | collective-permute-start | bytes 3145736 | tf_op jit(solution)/shard_map/ppermute | solution.py:295
  129.4 11.6 %collective-permute-start.6 = (f32[256,512]{1,0:T(8,128)}, f32[256,512]{1,0:T(8,128)}, u32[]{:S(2)}, u32[]{:S(2)}) collective-permute-start(f32[256,512]{1,0:T(8,128)} %add_select_fusion.own_ref), channel_id=1, source_target_pairs={{1,0},{2,1},{3,2},{0,3},{5,4},{6,5},{7,6},{4,7},{9,8},{10,9},{11,1... | collective-permute-start | bytes 1572872 | tf_op jit(solution)/shard_map/ppermute | solution.py:307
  134.0 14.2 %collective-permute-start.4 = (f32[256,512]{1,0:T(8,128)}, f32[256,512]{1,0:T(8,128)}, u32[]{:S(2)}, u32[]{:S(2)}) collective-permute-start(f32[256,512]{1,0:T(8,128)} %add_select_fusion.own_ref), channel_id=1, source_target_pairs={{0,1},{1,2},{2,3},{3,0},{4,5},{5,6},{6,7},{7,4},{8,9},{9,10},{10,1... | collective-permute-start | bytes 1572872 | tf_op jit(solution)/shard_map/ppermute | solution.py:306
  136.0 23.8 %collective-permute-start.13 = (f32[256,512]{1,0:T(8,128)}, f32[256,512]{1,0:T(8,128)}, u32[]{:S(2)}, u32[]{:S(2)}) collective-permute-start(f32[256,512]{1,0:T(8,128)} %bitcast.9.mine_ref), channel_id=1, source_target_pairs={{0,32},{32,0},{1,33},{33,1},{2,34},{34,2},{3,35},{35,3},{4,36},{36... | collective-permute-start | bytes 1572872 | tf_op jit(solution)/shard_map/ppermute | solution.py:280
  142.7 9.8 %collective-permute-start.7 = (f32[128,512]{1,0:T(8,128)}, f32[128,512]{1,0:T(8,128)S(1)}, u32[]{:S(2)}, u32[]{:S(2)}) collective-permute-start(f32[128,512]{1,0:T(8,128)} %slice.27), channel_id=1, source_target_pairs={{1,0},{2,1},{3,2},{0,3},{5,4},{6,5},{7,6},{4,7},{9,8},{10,9},{11,1... | collective-permute-start | bytes 786440 | tf_op jit(solution)/shard_map/ppermute | solution.py:310
  150.0 9.8 %collective-permute-start.5 = (f32[128,512]{1,0:T(8,128)}, f32[128,512]{1,0:T(8,128)}, u32[]{:S(2)}, u32[]{:S(2)}) collective-permute-start(f32[128,512]{1,0:T(8,128)} %slice.26), channel_id=1, source_target_pairs={{0,1},{1,2},{2,3},{3,0},{4,5},{5,6},{6,7},{7,4},{8,9},{9,10},{10,1... | collective-permute-start | bytes 786440 | tf_op jit(solution)/shard_map/ppermute | solution.py:309

commit v5 on v2

--- a/solution.py
+++ b/solution.py
@@ -96,30 +96,71 @@
         v_ref[there, :] -= _dot(v_ref[here, there].T, v_ref[here, :])
 
 
-def _factor_kernel(k, old_ref, v_ref):
+def _first_kernel(here_ref, old_ref, sent_ref, v_ref):
+    for value, ref in ((0, old_ref), (1, sent_ref)):
+
+        @pl.when(here_ref[2] == value)
+        def _():
+            v_ref[...] = ref[...]
+
+    _eliminate(0, v_ref)
+
+
+def _next_kernel(k, old_ref, v_ref):
     v_ref[...] = old_ref[...]
     _eliminate(k, v_ref)
 
 
-def factor_inverse(covariance):
-    state = covariance
-    for k in range(NB // BK):
+def _last_kernel(here_ref, old_ref, o_ref, v_ref):
+    _next_kernel(NB // BK - 1, old_ref, v_ref)
+    half = NB // 2
+    for value in range(2):
+
+        @pl.when(here_ref[2] == value)
+        def _():
+            o_ref[...] = v_ref[value * half : (value + 1) * half, :]
+
+
+def factor_inverse(here, covariance, sent):
+    whole = pl.BlockSpec((NB, NB), lambda i: (0, 0))
+    half = pl.BlockSpec((NB // 2, NB), lambda i: (0, 0))
+    scalars = pl.BlockSpec(memory_space=pltpu.SMEM)
+    rest = dict(
+        grid=(1,),
+        compiler_params=pltpu.CompilerParams(vmem_limit_bytes=24 * 2**20),
+        cost_estimate=pl.CostEstimate(flops=10**6, bytes_accessed=10**5, transcendentals=NB),
+    )
+    tile = jax.ShapeDtypeStruct((NB, NB), jnp.float32)
+    state = pl.pallas_call(
+        _first_kernel,
+        out_shape=tile,
+        in_specs=[scalars, whole, whole],
+        out_specs=whole,
+        name="factor_0",
+        **rest,
+    )(here, covariance, sent)
+    for k in range(1, NB // BK - 1):
         state = pl.pallas_call(
-            functools.partial(_factor_kernel, k),
-            grid=(1,),
-            out_shape=jax.ShapeDtypeStruct((NB, NB), jnp.float32),
-            in_specs=[pl.BlockSpec((NB, NB), lambda i: (0, 0))],
-            out_specs=pl.BlockSpec((NB, NB), lambda i: (0, 0)),
-            compiler_params=pltpu.CompilerParams(vmem_limit_bytes=24 * 2**20),
-            cost_estimate=pl.CostEstimate(flops=10**6, bytes_accessed=10**5, transcendentals=NB),
+            functools.partial(_next_kernel, k),
+            out_shape=tile,
+            in_specs=[whole],
+            out_specs=whole,
             name=f"factor_{k}",
+            **rest,
         )(state)
-    return state
-
-
-def _pick_kernel(which_ref, first_ref, *refs):
-    *others, o_ref, sem = refs
-    for i, ref in enumerate((first_ref.at[: o_ref.shape[0]], *others)):
+    return pl.pallas_call(
+        _last_kernel,
+        out_shape=jax.ShapeDtypeStruct((NB // 2, NB), jnp.float32),
+        in_specs=[scalars, whole],
+        out_specs=half,
+        scratch_shapes=[pltpu.VMEM((NB, NB), jnp.float32)],
+        name="factor_3",
+        **rest,
+    )(here, state)
+
+
+def _pick_kernel(which_ref, first_ref, second_ref, _, o_ref, sem):
+    for i, ref in enumerate((first_ref, second_ref)):
 
         @pl.when(which_ref[0] == i)
         def _():
@@ -128,17 +169,17 @@
             copy.wait()
 
 
-def pick(which, first, *others):
+def pick(which, first, second, after):
     return pl.pallas_call(
         _pick_kernel,
-        out_shape=jax.ShapeDtypeStruct(others[0].shape, jnp.float32),
+        out_shape=jax.ShapeDtypeStruct(first.shape, jnp.float32),
         in_specs=[pl.BlockSpec(memory_space=pltpu.SMEM)]
-        + [pl.BlockSpec(memory_space=pl.ANY)] * (1 + len(others)),
+        + [pl.BlockSpec(memory_space=pl.ANY)] * 3,
         out_specs=pl.BlockSpec(memory_space=pltpu.VMEM),
         scratch_shapes=[pltpu.SemaphoreType.DMA],
         cost_estimate=pl.CostEstimate(flops=0, bytes_accessed=10**6, transcendentals=0),
         name="pick",
-    )(which.reshape(1), first, *others)
+    )(which.reshape(1), first, second, after)
 
 
 def _split(value):
@@ -261,11 +302,10 @@
 def body(covariance):
     ny, nz, nx = (lax.axis_size(axis) for axis in ("y", "z", "x"))
     core, x, y, z = (lax.axis_index(axis) for axis in ("core", "x", "y", "z"))
-    half = NB // 2
     here = jnp.stack([y * 2 + core, z * nx + x, core, x]).astype(jnp.int32)
 
-    inverse = factor_inverse(covariance)
-    mine = pick(core, inverse, swap_cores(inverse[half:]))
+    tile = covariance[:NB]
+    mine = half = factor_inverse(here, covariance, lax.ppermute(tile, "core", [(0, 1)]))
     part = send_parts(mine, ("z", "x"), nz * nx)
     part = gather(part, "y", ny)[: part.shape[0]]
     mine = gather(part, ("z", "x"), nz * nx)
@@ -285,11 +325,15 @@
     top = lax.ppermute(back[:rest], "x", ring)
     low = lax.ppermute(ahead[rest:], "x", back_ring)
 
-    mirror = covariance[:NB]
+    mirror = tile
     for step in (4, 2, 1):
         pairs = [(2 * i, 2 * (i + step)) for i in range(0, ny, 2 * step)]
         sent = lax.ppermute(mirror, ("y", "core"), pairs)
-        mirror = jnp.where(y % (2 * step) == step, sent, mirror)
+        here_now = y % (2 * step) == step
+        if step == 4:
+            mirror = pick(here_now.astype(jnp.int32), mirror, sent, after=half)
+        else:
+            mirror = jnp.where(here_now, sent, mirror)
     mirror = mirror, lax.ppermute(mirror, "core", [(0, 1)])
     return update(here, covariance, (own, back, top, low, ahead), mirror, inverse)
 

time: 150 us -> 146 us (0.973)
  waiting for transfers between devices: 25.4 us -> 19.3 us
  starting transfers between devices: 75 us -> 77 us
    all_to_all x2, waiting for transfers between devices: 9.86 us -> 4.77 us  [send_parts(): lax.all_to_all(value.reshape(parts, size, value.shape[1]), axis, 0, 0)[0]]
    all_to_all x2, waiting for transfers between devices: 6.7 us -> 4.55 us  [gather(): return lax.all_to_all(copies, axis, 0, 0).reshape(-1, value.shape[1])]
    slice x2 -> x1, local copies, waits for them, and re-layouts: 3.14 us -> 1.04 us  [body(): tile = covariance[:NB]]
    ppermute x2 -> x1, starting transfers between devices: 3.82 us -> 1.91 us  [swap_cores(): return lax.ppermute(value, 'core', [(0, 1), (1, 0)])]
    ppermute x0 -> x1, starting transfers between devices: none -> 1.79 us  [body(): lax.ppermute(tile, 'core', [(0, 1)])]
    all_to_all x2, starting transfers between devices: 19.2 us -> 20.7 us  [gather(): return lax.all_to_all(copies, axis, 0, 0).reshape(-1, value.shape[1])]
    select_n x3 -> x2, other arithmetic: 4.07 us -> 2.88 us  [body(): mirror = jnp.where(here_now, sent, mirror)]
  transfers between devices with their start and end apart: 18 -> 18, of which waited for: 6 -> 6; matrix products, arithmetic and copies ran while one was open for 9% -> 10% of each run, Pallas kernels for 16% -> 17%
where the time goes in v5:
time: 146 us; the launch traced here: 145 us
  starting transfers between devices  77 us (53%)
  Pallas kernels  33.7 us (23%)
  waiting for transfers between devices  19.3 us (13%)
  other arithmetic  7.37 us (5%)
  local copies, waits for them, and re-layouts  7.13 us (5%)
    all_to_all x2, starting transfers between devices, gather(): return lax.all_to_all(copies, axis, 0, 0).reshape(-1, value.shape[1])  20.7 us
    all_to_all x2, starting transfers between devices, send_parts(): lax.all_to_all(value.reshape(parts, size, value.shape[1]), axis, 0, 0)[0]  17.4 us
    ppermute x3, starting transfers between devices, body(): sent = lax.ppermute(mirror, ('y', 'core'), pairs)  13.3 us
    pallas_call x2, Pallas kernels, factor_inverse(): pl.pallas_call(functools.partial(_next_kernel, k), out_shape=tile, in_spe...  10.3 us
    pallas_call x1, Pallas kernels, update(): pl.pallas_call(_update_kernel, grid=(state.shape[0] // CHUNK,), out_shape...  8.75 us
    ppermute x1, waiting for transfers between devices, body(): top = lax.ppermute(back[:rest], 'x', ring)  6.59 us
    pallas_call x1, Pallas kernels, factor_inverse(): pl.pallas_call(_last_kernel, out_shape=jax.ShapeDtypeStruct((NB // 2, NB)...  6.25 us
    pallas_call x1, Pallas kernels, factor_inverse(): pl.pallas_call(_first_kernel, out_shape=tile, in_specs=[scalars, whole, w...  6.24 us
  transfers between devices with their start and end apart: 18, of which 6 were waited for; matrix products, arithmetic and copies ran while one was open for 10% of the time, Pallas kernels for 17%

profile of v5, /device:TPU:64, one launch (start us, length us, event | category | flops | bytes accessed | tf_op | source)
XLA Modules:
  0.0 145.0 jit_solution(96175569142750663)
XLA Ops:
  0.0 4.6 %all-to-all-start = ((f32[4,256,512]{2,1,0:T(8,128)}), f32[4,256,512]{2,1,0:T(8,128)}, u32[]{:S(2)}, u32[]{:S(2)}) async-start(f32[4,256,512]{2,1,0:T(8,128)} %bitcast.16), calls=%async_computation | async-start | bytes 4194304 | tf_op jit(solution)/shard_map/all_to_all | solution.py:290
  4.6 1.0 slice.22.first_ref
  5.6 1.8 %collective-permute-start.9 = (f32[512,512]{1,0:T(8,128)}, f32[512,512]{1,0:T(8,128)S(1)}, u32[]{:S(2)}, u32[]{:S(2)}) collective-permute-start(f32[512,512]{1,0:T(8,128)} %slice.22.first_ref), channel_id=1, source_target_pairs={{0,32},{1,33},{2,34},{3,35},{4,36},{5,37},{6,38},{7,39},{8,40},{9,... | collective-permute-start | bytes 3145736 | tf_op jit(solution)/shard_map/ppermute | solution.py:308
  7.4 8.7 %collective-permute-start.8 = (f32[512,512]{1,0:T(8,128)}, f32[512,512]{1,0:T(8,128)}, u32[]{:S(2)}, u32[]{:S(2)}) collective-permute-start(f32[512,512]{1,0:T(8,128)} %slice.22.first_ref), channel_id=1, source_target_pairs={{0,256},{1,257},{2,258},{3,259},{4,260},{5,261},{6,262},{7,263},{8... | collective-permute-start | bytes 3145736 | tf_op jit(solution)/shard_map/ppermute | solution.py:331
  16.2 0.1 pad_add_fusion.here_ref
  16.2 0.0 collective-permute-done.9.sent_ref
  16.2 6.2 %factor_0.1.old_ref = f32[512,512]{1,0:T(8,128)S(1)} custom-call(s32[4]{0:T(128)S(1)} %pad_add_fusion.here_ref, f32[1024,512]{1,0:T(8,128)S(1)} %copy-done, f32[512,512]{1,0:T(8,128)S(1)} %collective-permute-done.9.sent_ref), custom_call_target="tpu_custom_call" | custom-call | flops 1000000 | bytes 100000 | tf_op jit(solution)/shard_map/factor_0/pallas_call | solution.py:134
  22.5 5.3 %factor_1.1.old_ref = f32[512,512]{1,0:T(8,128)S(1)} custom-call(f32[512,512]{1,0:T(8,128)S(1)} %factor_0.1.old_ref), custom_call_target="tpu_custom_call" | custom-call | flops 1000000 | bytes 100000 | tf_op jit(solution)/shard_map/factor_1/pallas_call | solution.py:143
  27.8 5.0 %factor_2.1.old_ref = f32[512,512]{1,0:T(8,128)S(1)} custom-call(f32[512,512]{1,0:T(8,128)S(1)} %factor_1.1.old_ref), custom_call_target="tpu_custom_call" | custom-call | flops 1000000 | bytes 100000 | tf_op jit(solution)/shard_map/factor_2/pallas_call | solution.py:143
  32.8 6.2 %factor_3.1._ = f32[256,512]{1,0:T(8,128)} custom-call(s32[4]{0:T(128)S(1)} %pad_add_fusion.here_ref, f32[512,512]{1,0:T(8,128)S(1)} %factor_2.1.old_ref), custom_call_target="tpu_custom_call" | custom-call | flops 1000000 | bytes 100000 | tf_op jit(solution)/shard_map/factor_3/pallas_call | solution.py:151
  39.1 0.0 collective-permute-done.8.second_ref
  39.1 2.2 %pick.1 = f32[512,512]{1,0:T(8,128)} custom-call(s32[1]{0:T(128)} %bitcast.6.which_ref, f32[512,512]{1,0:T(8,128)} %slice.22.first_ref, f32[512,512]{1,0:T(8,128)} %collective-permute-done.8.second_ref, f32[256,512]{1,0:T(8,128)} %factor_3.1._), custom_call_target="tpu_custom_call" | custom-call | bytes 1000000 | tf_op jit(solution)/shard_map/pick/pallas_call | solution.py:173
  41.3 2.3 %collective-permute-start.10 = (f32[512,512]{1,0:T(8,128)}, f32[512,512]{1,0:T(8,128)}, u32[]{:S(2)}, u32[]{:S(2)}) collective-permute-start(f32[512,512]{1,0:T(8,128)} %pick.1), channel_id=1, source_target_pairs={{0,128},{256,384},{1,129},{257,385},{2,130},{258,386},{3,131},{259... | collective-permute-start | bytes 3145736 | tf_op jit(solution)/shard_map/ppermute | solution.py:331
  43.6 12.8 %all-to-all-start.1 = ((f32[32,8,512]{2,1,0:T(8,128)}), f32[32,8,512]{2,1,0:T(8,128)}, u32[]{:S(2)}, u32[]{:S(2)}) async-start(f32[32,8,512]{2,1,0:T(8,128)} %bitcast.7), calls=%async_computation.1 | async-start | bytes 1048576 | tf_op jit(solution)/shard_map/all_to_all | solution.py:290
  56.4 1.9 %slice_bitcast_fusion = f32[256,512]{1,0:T(8,128)} fusion(f32[4,256,512]{2,1,0:T(8,128)} %all-to-all-done), kind=kLoop, calls=%fused_computation | loop fusion | bytes 1048576 | tf_op jit(solution)/shard_map/squeeze | solution.py:290
  58.3 1.5 %collective-permute-start.1 = (f32[256,512]{1,0:T(8,128)}, f32[256,512]{1,0:T(8,128)}, u32[]{:S(2)}, u32[]{:S(2)}) collective-permute-start(f32[256,512]{1,0:T(8,128)} %slice_bitcast_fusion), channel_id=1, source_target_pairs={{0,20},{1,21},{2,22},{3,23},{32,52},{33,53},{34,54},{35,55},{64,84... | collective-permute-start | bytes 1572872 | tf_op jit(solution)/shard_map/ppermute | solution.py:315
  59.7 1.4 collective-permute-start
  61.2 0.0 collective-permute-done.10
  61.2 1.4 broadcast_select_fusion
  62.6 0.0 copy-start.1
  62.6 2.3 %collective-permute-start.11 = (f32[512,512]{1,0:T(8,128)S(1)}, f32[512,512]{1,0:T(8,128)}, u32[]{:S(2)}, u32[]{:S(2)}) collective-permute-start(f32[512,512]{1,0:T(8,128)S(1)} %broadcast_select_fusion), channel_id=1, source_target_pairs={{0,64},{128,192},{256,320},{384,448},{1,65},{129,193},{257,321},{3... | collective-permute-start | bytes 3145736 | tf_op jit(solution)/shard_map/ppermute | solution.py:331
  64.9 4.8 %all-to-all-done.1 = f32[32,8,512]{2,1,0:T(8,128)} async-done(((f32[32,8,512]{2,1,0:T(8,128)}), f32[32,8,512]{2,1,0:T(8,128)}, u32[]{:S(2)}, u32[]{:S(2)}) %all-to-all-start.1) | async-done | bytes 524320 | tf_op jit(solution)/shard_map/all_to_all | solution.py:290
  69.7 0.7 slice_bitcast_fusion.2
  70.4 0.7 broadcast_in_dim.16
  71.1 4.5 %all-to-all-start.2 = ((f32[8,8,512]{2,1,0:T(8,128)}), f32[8,8,512]{2,1,0:T(8,128)S(1)}, u32[]{:S(2)}, u32[]{:S(2)}) async-start(f32[8,8,512]{2,1,0:T(8,128)} %broadcast_in_dim.16), calls=%async_computation.2 | async-start | bytes 262144 | tf_op jit(solution)/shard_map/all_to_all | solution.py:295
  75.6 0.0 collective-permute-done.1
  75.6 0.0 collective-permute-done
  75.6 2.3 %add_select_fusion.1 = f32[256,512]{1,0:T(8,128)} fusion(f32[256,512]{1,0:T(8,128)} %collective-permute-done, f32[256,512]{1,0:T(8,128)} %collective-permute-done.1, pred[]{:T(512)S(6)} %eq.23, f32[4,256,512]{2,1,0:T(8,128)} %all-to-all-done), kind=kLoop, calls=%fused_computation.2 | loop fusion | flops 262144 | bytes 2097153 | tf_op jit(solution)/shard_map/jit(_where)/select_n | solution.py:316
  77.9 1.5 %collective-permute-start.3 = (f32[256,512]{1,0:T(8,128)}, f32[256,512]{1,0:T(8,128)}, u32[]{:S(2)}, u32[]{:S(2)}) collective-permute-start(f32[256,512]{1,0:T(8,128)} %add_select_fusion.1), channel_id=1, source_target_pairs={{0,28},{12,8},{1,29},{13,9},{2,30},{14,10},{3,31},{15,11},{32,60},... | collective-permute-start | bytes 1572872 | tf_op jit(solution)/shard_map/ppermute | solution.py:318
  79.3 1.3 collective-permute-start.2
  80.6 3.8 %all-to-all-done.2 = f32[8,8,512]{2,1,0:T(8,128)S(1)} async-done(((f32[8,8,512]{2,1,0:T(8,128)}), f32[8,8,512]{2,1,0:T(8,128)S(1)}, u32[]{:S(2)}, u32[]{:S(2)}) %all-to-all-start.2) | async-done | bytes 131104 | tf_op jit(solution)/shard_map/all_to_all | solution.py:295
  84.5 0.9 broadcast_in_dim.18
  85.4 16.2 %all-to-all-start.3 = ((f32[32,8,512]{2,1,0:T(8,128)}), f32[32,8,512]{2,1,0:T(8,128)}, u32[]{:S(2)}, u32[]{:S(2)}) async-start(f32[32,8,512]{2,1,0:T(8,128)} %broadcast_in_dim.18), calls=%async_computation.3 | async-start | bytes 1048576 | tf_op jit(solution)/shard_map/all_to_all | solution.py:295
  101.6 1.4 broadcast_select_fusion.1.tile_ref
  103.1 2.3 %collective-permute-start.12 = (f32[512,512]{1,0:T(8,128)S(1)}, f32[512,512]{1,0:T(8,128)}, u32[]{:S(2)}, u32[]{:S(2)}) collective-permute-start(f32[512,512]{1,0:T(8,128)S(1)} %broadcast_select_fusion.1.tile_ref), channel_id=1, source_target_pairs={{0,32},{1,33},{2,34},{3,35},{4,36},{5,37},{6,38},{7,39},{8,40},{9,... | collective-permute-start | bytes 3145736 | tf_op jit(solution)/shard_map/ppermute | solution.py:337
  105.4 2.1 %add_select_fusion.own_ref = f32[256,512]{1,0:T(8,128)} fusion(f32[256,512]{1,0:T(8,128)} %add_select_fusion.1, f32[256,512]{1,0:T(8,128)} %collective-permute-done.2, f32[256,512]{1,0:T(8,128)} %collective-permute-done.3, pred[]{:T(512)S(6)} %or.7), kind=kLoop, calls=%fused_computation.1 | loop fusion | flops 262144 | bytes 2097153 | tf_op jit(solution)/shard_map/jit(_where)/select_n | solution.py:319
  107.5 4.6 %collective-permute-start.6 = (f32[256,512]{1,0:T(8,128)}, f32[256,512]{1,0:T(8,128)}, u32[]{:S(2)}, u32[]{:S(2)}) collective-permute-start(f32[256,512]{1,0:T(8,128)} %add_select_fusion.own_ref), channel_id=1, source_target_pairs={{1,0},{2,1},{3,2},{0,3},{5,4},{6,5},{7,6},{4,7},{9,8},{10,9},{11,1... | collective-permute-start | bytes 1572872 | tf_op jit(solution)/shard_map/ppermute | solution.py:323
  112.1 1.9 %collective-permute-start.4 = (f32[256,512]{1,0:T(8,128)}, f32[256,512]{1,0:T(8,128)}, u32[]{:S(2)}, u32[]{:S(2)}) collective-permute-start(f32[256,512]{1,0:T(8,128)} %add_select_fusion.own_ref), channel_id=1, source_target_pairs={{0,1},{1,2},{2,3},{3,0},{4,5},{5,6},{6,7},{7,4},{8,9},{9,10},{10,1... | collective-permute-start | bytes 1572872 | tf_op jit(solution)/shard_map/ppermute | solution.py:322
  114.0 0.7 all-to-all-done.3
  114.7 1.9 %collective-permute-start.13 = (f32[256,512]{1,0:T(8,128)}, f32[256,512]{1,0:T(8,128)S(1)}, u32[]{:S(2)}, u32[]{:S(2)}) collective-permute-start(f32[256,512]{1,0:T(8,128)} %bitcast.10.mine_ref), channel_id=1, source_target_pairs={{0,32},{32,0},{1,33},{33,1},{2,34},{34,2},{3,35},{35,3},{4,36},{36... | collective-permute-start | bytes 1572872 | tf_op jit(solution)/shard_map/ppermute | solution.py:299
  116.6 2.4 %collective-permute-done.6.ahead_ref = f32[256,512]{1,0:T(8,128)} collective-permute-done((f32[256,512]{1,0:T(8,128)}, f32[256,512]{1,0:T(8,128)}, u32[]{:S(2)}, u32[]{:S(2)}) %collective-permute-start.6) | collective-permute-done | bytes 524320 | tf_op jit(solution)/shard_map/ppermute | solution.py:323
  119.1 1.0 slice.27
  120.0 5.6 %collective-permute-start.7 = (f32[128,512]{1,0:T(8,128)S(1)}, f32[128,512]{1,0:T(8,128)S(1)}, u32[]{:S(2)}, u32[]{:S(2)}) collective-permute-start(f32[128,512]{1,0:T(8,128)S(1)} %slice.27), channel_id=1, source_target_pairs={{1,0},{2,1},{3,2},{0,3},{5,4},{6,5},{7,6},{4,7},{9,8},{10,9},{11,1... | collective-permute-start | bytes 786440 | tf_op jit(solution)/shard_map/ppermute | solution.py:326
  125.7 1.0 slice.26
  126.6 1.9 %collective-permute-start.5 = (f32[128,512]{1,0:T(8,128)S(1)}, f32[128,512]{1,0:T(8,128)S(1)}, u32[]{:S(2)}, u32[]{:S(2)}) collective-permute-start(f32[128,512]{1,0:T(8,128)S(1)} %slice.26), channel_id=1, source_target_pairs={{0,1},{1,2},{2,3},{3,0},{4,5},{5,6},{6,7},{7,4},{8,9},{9,10},{10,1... | collective-permute-start | bytes 786440 | tf_op jit(solution)/shard_map/ppermute | solution.py:325
  128.6 1.0 collective-permute-done.7.low_ref
  129.5 6.6 %collective-permute-done.5.top_ref = f32[128,512]{1,0:T(8,128)S(1)} collective-permute-done((f32[128,512]{1,0:T(8,128)S(1)}, f32[128,512]{1,0:T(8,128)S(1)}, u32[]{:S(2)}, u32[]{:S(2)}) %collective-permute-start.5) | collective-permute-done | bytes 262176 | tf_op jit(solution)/shard_map/ppermute | solution.py:325
  136.1 8.7 %update.1 = f32[1024,512]{1,0:T(8,128)} custom-call(s32[4]{0:T(128)S(1)} %pad_add_fusion.here_ref, f32[1024,512]{1,0:T(8,128)S(1)} %copy-done, f32[256,512]{1,0:T(8,128)} %add_select_fusion.own_ref, f32[256,512]{1,0:T(8,128)} %collective-permute-done.4.back_ref, f32[128,512]{1,0:T(8,128)S(1)} %collective-permute-done.5.top_ref, ...), custom_call_target="tpu_custom_call" | custom-call | flops 4026531840 | bytes 8388608 | tf_op jit(solution)/shard_map/update/pallas_call | solution.py:264
  (11 shorter events, 0.0 us)
Async XLA Ops:
  0.0 4.6 %copy-start = (f32[1024,512]{1,0:T(8,128)S(1)}, f32[1024,512]{1,0:T(8,128)}, u32[]{:S(2)}) copy-start(f32[1024,512]{1,0:T(8,128)} %state_ref.1) | copy-start | bytes 6291460
  0.0 43.6 %all-to-all-start = ((f32[4,256,512]{2,1,0:T(8,128)}), f32[4,256,512]{2,1,0:T(8,128)}, u32[]{:S(2)}, u32[]{:S(2)}) async-start(f32[4,256,512]{2,1,0:T(8,128)} %bitcast.16), calls=%async_computation | async-start | bytes 4194304 | tf_op jit(solution)/shard_map/all_to_all | solution.py:290
  5.6 10.6 %collective-permute-start.9 = (f32[512,512]{1,0:T(8,128)}, f32[512,512]{1,0:T(8,128)S(1)}, u32[]{:S(2)}, u32[]{:S(2)}) collective-permute-start(f32[512,512]{1,0:T(8,128)} %slice.22.first_ref), channel_id=1, source_target_pairs={{0,32},{1,33},{2,34},{3,35},{4,36},{5,37},{6,38},{7,39},{8,40},{9,... | collective-permute-start | bytes 3145736 | tf_op jit(solution)/shard_map/ppermute | solution.py:308
  7.4 31.6 %collective-permute-start.8 = (f32[512,512]{1,0:T(8,128)}, f32[512,512]{1,0:T(8,128)}, u32[]{:S(2)}, u32[]{:S(2)}) collective-permute-start(f32[512,512]{1,0:T(8,128)} %slice.22.first_ref), channel_id=1, source_target_pairs={{0,256},{1,257},{2,258},{3,259},{4,260},{5,261},{6,262},{7,263},{8... | collective-permute-start | bytes 3145736 | tf_op jit(solution)/shard_map/ppermute | solution.py:331
  41.3 19.9 %collective-permute-start.10 = (f32[512,512]{1,0:T(8,128)}, f32[512,512]{1,0:T(8,128)}, u32[]{:S(2)}, u32[]{:S(2)}) collective-permute-start(f32[512,512]{1,0:T(8,128)} %pick.1), channel_id=1, source_target_pairs={{0,128},{256,384},{1,129},{257,385},{2,130},{258,386},{3,131},{259... | collective-permute-start | bytes 3145736 | tf_op jit(solution)/shard_map/ppermute | solution.py:331
  43.6 26.1 %all-to-all-start.1 = ((f32[32,8,512]{2,1,0:T(8,128)}), f32[32,8,512]{2,1,0:T(8,128)}, u32[]{:S(2)}, u32[]{:S(2)}) async-start(f32[32,8,512]{2,1,0:T(8,128)} %bitcast.7), calls=%async_computation.1 | async-start | bytes 1048576 | tf_op jit(solution)/shard_map/all_to_all | solution.py:290
  58.3 17.3 %collective-permute-start.1 = (f32[256,512]{1,0:T(8,128)}, f32[256,512]{1,0:T(8,128)}, u32[]{:S(2)}, u32[]{:S(2)}) collective-permute-start(f32[256,512]{1,0:T(8,128)} %slice_bitcast_fusion), channel_id=1, source_target_pairs={{0,20},{1,21},{2,22},{3,23},{32,52},{33,53},{34,54},{35,55},{64,84... | collective-permute-start | bytes 1572872 | tf_op jit(solution)/shard_map/ppermute | solution.py:315
  59.7 15.8 %collective-permute-start = (f32[256,512]{1,0:T(8,128)}, f32[256,512]{1,0:T(8,128)}, u32[]{:S(2)}, u32[]{:S(2)}) collective-permute-start(f32[256,512]{1,0:T(8,128)} %slice_bitcast_fusion), channel_id=1, source_target_pairs={{0,12},{1,13},{2,14},{3,15},{32,44},{33,45},{34,46},{35,47},{64,76... | collective-permute-start | bytes 1572872 | tf_op jit(solution)/shard_map/ppermute | solution.py:315
  62.6 39.0 %copy-start.1 = (f32[512,512]{1,0:T(8,128)}, f32[512,512]{1,0:T(8,128)S(1)}, u32[]{:S(2)}) copy-start(f32[512,512]{1,0:T(8,128)S(1)} %broadcast_select_fusion) | copy-start | bytes 3145732
  62.6 39.0 %collective-permute-start.11 = (f32[512,512]{1,0:T(8,128)S(1)}, f32[512,512]{1,0:T(8,128)}, u32[]{:S(2)}, u32[]{:S(2)}) collective-permute-start(f32[512,512]{1,0:T(8,128)S(1)} %broadcast_select_fusion), channel_id=1, source_target_pairs={{0,64},{128,192},{256,320},{384,448},{1,65},{129,193},{257,321},{3... | collective-permute-start | bytes 3145736 | tf_op jit(solution)/shard_map/ppermute | solution.py:331
  71.1 13.4 %all-to-all-start.2 = ((f32[8,8,512]{2,1,0:T(8,128)}), f32[8,8,512]{2,1,0:T(8,128)S(1)}, u32[]{:S(2)}, u32[]{:S(2)}) async-start(f32[8,8,512]{2,1,0:T(8,128)} %broadcast_in_dim.16), calls=%async_computation.2 | async-start | bytes 262144 | tf_op jit(solution)/shard_map/all_to_all | solution.py:295
  77.9 27.5 %collective-permute-start.3 = (f32[256,512]{1,0:T(8,128)}, f32[256,512]{1,0:T(8,128)}, u32[]{:S(2)}, u32[]{:S(2)}) collective-permute-start(f32[256,512]{1,0:T(8,128)} %add_select_fusion.1), channel_id=1, source_target_pairs={{0,28},{12,8},{1,29},{13,9},{2,30},{14,10},{3,31},{15,11},{32,60},... | collective-permute-start | bytes 1572872 | tf_op jit(solution)/shard_map/ppermute | solution.py:318
  79.3 26.0 %collective-permute-start.2 = (f32[256,512]{1,0:T(8,128)}, f32[256,512]{1,0:T(8,128)}, u32[]{:S(2)}, u32[]{:S(2)}) collective-permute-start(f32[256,512]{1,0:T(8,128)} %add_select_fusion.1), channel_id=1, source_target_pairs={{0,4},{12,16},{20,24},{1,5},{13,17},{21,25},{2,6},{14,18},{22,26},... | collective-permute-start | bytes 1572872 | tf_op jit(solution)/shard_map/ppermute | solution.py:317
  85.4 29.3 %all-to-all-start.3 = ((f32[32,8,512]{2,1,0:T(8,128)}), f32[32,8,512]{2,1,0:T(8,128)}, u32[]{:S(2)}, u32[]{:S(2)}) async-start(f32[32,8,512]{2,1,0:T(8,128)} %broadcast_in_dim.18), calls=%async_computation.3 | async-start | bytes 1048576 | tf_op jit(solution)/shard_map/all_to_all | solution.py:295
  103.1 33.0 %collective-permute-start.12 = (f32[512,512]{1,0:T(8,128)S(1)}, f32[512,512]{1,0:T(8,128)}, u32[]{:S(2)}, u32[]{:S(2)}) collective-permute-start(f32[512,512]{1,0:T(8,128)S(1)} %broadcast_select_fusion.1.tile_ref), channel_id=1, source_target_pairs={{0,32},{1,33},{2,34},{3,35},{4,36},{5,37},{6,38},{7,39},{8,40},{9,... | collective-permute-start | bytes 3145736 | tf_op jit(solution)/shard_map/ppermute | solution.py:337
  107.5 11.6 %collective-permute-start.6 = (f32[256,512]{1,0:T(8,128)}, f32[256,512]{1,0:T(8,128)}, u32[]{:S(2)}, u32[]{:S(2)}) collective-permute-start(f32[256,512]{1,0:T(8,128)} %add_select_fusion.own_ref), channel_id=1, source_target_pairs={{1,0},{2,1},{3,2},{0,3},{5,4},{6,5},{7,6},{4,7},{9,8},{10,9},{11,1... | collective-permute-start | bytes 1572872 | tf_op jit(solution)/shard_map/ppermute | solution.py:323
  112.1 13.6 %collective-permute-start.4 = (f32[256,512]{1,0:T(8,128)}, f32[256,512]{1,0:T(8,128)}, u32[]{:S(2)}, u32[]{:S(2)}) collective-permute-start(f32[256,512]{1,0:T(8,128)} %add_select_fusion.own_ref), channel_id=1, source_target_pairs={{0,1},{1,2},{2,3},{3,0},{4,5},{5,6},{6,7},{7,4},{8,9},{9,10},{10,1... | collective-permute-start | bytes 1572872 | tf_op jit(solution)/shard_map/ppermute | solution.py:322
  114.7 21.4 %collective-permute-start.13 = (f32[256,512]{1,0:T(8,128)}, f32[256,512]{1,0:T(8,128)S(1)}, u32[]{:S(2)}, u32[]{:S(2)}) collective-permute-start(f32[256,512]{1,0:T(8,128)} %bitcast.10.mine_ref), channel_id=1, source_target_pairs={{0,32},{32,0},{1,33},{33,1},{2,34},{34,2},{3,35},{35,3},{4,36},{36... | collective-permute-start | bytes 1572872 | tf_op jit(solution)/shard_map/ppermute | solution.py:299
  120.0 9.5 %collective-permute-start.7 = (f32[128,512]{1,0:T(8,128)S(1)}, f32[128,512]{1,0:T(8,128)S(1)}, u32[]{:S(2)}, u32[]{:S(2)}) collective-permute-start(f32[128,512]{1,0:T(8,128)S(1)} %slice.27), channel_id=1, source_target_pairs={{1,0},{2,1},{3,2},{0,3},{5,4},{6,5},{7,6},{4,7},{9,8},{10,9},{11,1... | collective-permute-start | bytes 786440 | tf_op jit(solution)/shard_map/ppermute | solution.py:326
  126.6 9.5 %collective-permute-start.5 = (f32[128,512]{1,0:T(8,128)S(1)}, f32[128,512]{1,0:T(8,128)S(1)}, u32[]{:S(2)}, u32[]{:S(2)}) collective-permute-start(f32[128,512]{1,0:T(8,128)S(1)} %slice.26), channel_id=1, source_target_pairs={{0,1},{1,2},{2,3},{3,0},{4,5},{5,6},{6,7},{7,4},{8,9},{9,10},{10,1... | collective-permute-start | bytes 786440 | tf_op jit(solution)/shard_map/ppermute | solution.py:325
